TPU v7x, 256 devices: a whole 4x4x8 slice. The times are simulated.
256 devices in a mesh: dp: 8 (over z), sp: 32 (over y, x, core).
Axes of the slice: x: 4, y: 4, z: 8, core: 2. Of those that a mesh axis runs over, the one named last changes fastest.
Arguments:
- tokens: bfloat16 [65536, 2048], P(('dp', 'sp')), may hold values from -9 to 9
- qkv_weight: bfloat16 [2048, 3072], P(('dp', 'sp')), may hold values from -0.125 to 0.125
- route: int32 [65536], P(('dp', 'sp')), may hold values from 0 to 7, as said below
- offset: int32 [65536], P(('dp', 'sp')), may hold values from 0 to 8191, as said below
- doc_lengths: int32 [8, 16], P('dp'), may hold values from 1 to 2048, 8192 in all within a row
Outputs:
- attended: bfloat16 [65536, 2048], P(('dp', 'sp'))
Inputs may be any that keep to these rules, and one draw needn't show every extreme that they name: `route`: at every sp index the loader tokens of all dp indices map one to one onto the group rows of that sp index; every device sends 64 rows to one group, none to another and 32 to each other group. offset // 256 is the sp index of the token's device; no two tokens share route and offset.
All inputs are finite; a program needn't handle non-finite values.
Results may differ from a plain program's by a relative error of at most 0.012.
The roundings to bfloat16 on the way count: a program that leaves them out, or rounds other values in their place, can miss the bound.
Values may be sent and summed in bfloat16 or wider, within the bound.
A program may use at most 64 MiB of HBM per device.

v0:
```python
import jax
import jax.numpy as jnp
from jax import lax
from jax.sharding import PartitionSpec as P

QUERY_HEADS = 16
KEY_VALUE_HEADS = 4
HEAD_SIZE = 128


ROPE_BASE = 500000.0


def doc_positions(points, lens):
    ends = jnp.cumsum(lens)
    doc = jnp.sum((points[:, None] >= ends[None, :]).astype(jnp.int32), axis=1)
    starts = ends - lens
    picks = jnp.arange(lens.shape[0], dtype=jnp.int32)
    first = jnp.sum(jnp.where(doc[:, None] == picks[None, :], starts[None, :], 0), axis=1)
    return (doc, points - first)


def rotate(value_rows_local, pos):
    half = value_rows_local.shape[-1] // 2
    freq = ROPE_BASE ** (-(jnp.arange(half, dtype=jnp.float32) * 2.0 / value_rows_local.shape[-1]))
    angle = pos.astype(jnp.float32)[:, None] * freq[None, :]
    cosine = jnp.cos(angle)[:, None, :]
    sine = jnp.sin(angle)[:, None, :]
    first, second = (value_rows_local[..., :half], value_rows_local[..., half:])
    return jnp.concatenate(
        [first * cosine - second * sine, second * cosine + first * sine], axis=-1
    )


def on_device(tokens, qkv_weight, route, offset, doc_lengths):
    n_dp = lax.axis_size("dp")
    sequence_ranks = lax.axis_size("sp")
    sp_idx = lax.axis_index("sp")
    token_rows = tokens.shape[0]
    capacity = 2 * token_rows // n_dp
    local_slot = offset - sp_idx * token_rows
    onehot = (route[:, None] == jnp.arange(n_dp, dtype=jnp.int32)[None, :]).astype(jnp.int32)
    rank = jnp.sum((jnp.cumsum(onehot, axis=0) - onehot) * onehot, axis=1)
    where_to = route * capacity + rank
    feats = tokens.shape[1]
    buffer = jnp.zeros((n_dp * capacity, feats), tokens.dtype).at[where_to].set(tokens)
    slots = jnp.full((n_dp * capacity,), token_rows, jnp.int32).at[where_to].set(local_slot)
    landed = lax.all_to_all(
        buffer.reshape(n_dp, capacity, feats), "dp", split_axis=0, concat_axis=0, tiled=True
    )
    landed_slots = lax.all_to_all(
        slots.reshape(n_dp, capacity), "dp", split_axis=0, concat_axis=0, tiled=True
    )
    placed = jnp.zeros((token_rows, feats), tokens.dtype)
    inputs = placed.at[landed_slots.reshape(-1)].set(
        landed.reshape(n_dp * capacity, feats), mode="drop"
    )
    query_key_value = jnp.dot(
        inputs,
        lax.all_gather(qkv_weight, ("dp", "sp"), axis=0, tiled=True),
        preferred_element_type=jnp.float32,
    ).astype(jnp.bfloat16)
    lens = doc_lengths[0]
    points = sp_idx * token_rows + jnp.arange(token_rows, dtype=jnp.int32)
    seq_doc, seq_pos = doc_positions(points, lens)
    query_width = QUERY_HEADS * HEAD_SIZE
    query = query_key_value[:, :query_width].reshape(token_rows, QUERY_HEADS, HEAD_SIZE)
    key_rows_local = query_key_value[
        :, query_width : query_width + KEY_VALUE_HEADS * HEAD_SIZE
    ].reshape(token_rows, KEY_VALUE_HEADS, HEAD_SIZE)
    value_rows_local = query_key_value[:, query_width + KEY_VALUE_HEADS * HEAD_SIZE :].reshape(
        token_rows, KEY_VALUE_HEADS, HEAD_SIZE
    )
    query = rotate(query.astype(jnp.float32), seq_pos).astype(jnp.bfloat16)
    key_rows_local = rotate(key_rows_local.astype(jnp.float32), seq_pos).astype(jnp.bfloat16)
    splits = max(1, sequence_ranks // QUERY_HEADS)
    units = QUERY_HEADS * splits // sequence_ranks
    part_rows = token_rows // splits
    query_send = jnp.transpose(
        query.reshape(splits, part_rows, QUERY_HEADS, HEAD_SIZE), (2, 0, 1, 3)
    ).reshape(QUERY_HEADS * splits, part_rows, HEAD_SIZE)
    partner_rows = jnp.concatenate([key_rows_local, value_rows_local], axis=-1)
    partner_outbound = jnp.transpose(
        jnp.repeat(partner_rows, sequence_ranks // KEY_VALUE_HEADS, axis=1), (1, 0, 2)
    )
    query_got, paired_got = (
        lax.all_to_all(query_send, "sp", split_axis=0, concat_axis=1, tiled=True),
        lax.all_to_all(partner_outbound, "sp", split_axis=0, concat_axis=1, tiled=True),
    )
    group = sequence_ranks * token_rows
    longest = min(2048, group // 4)
    qcount = group // splits
    unit_ids = sp_idx * units + jnp.arange(units, dtype=jnp.int32)
    within = jnp.arange(qcount, dtype=jnp.int32)
    query_points = (
        within[None, :] // part_rows * token_rows
        + unit_ids[:, None] % splits * part_rows
        + within[None, :] % part_rows
    )
    query_points = query_points.reshape(units * qcount)
    query_doc, query_pos = doc_positions(query_points, lens)
    key_points = jnp.arange(group, dtype=jnp.int32)
    key_doc, unused_keypos = doc_positions(key_points, lens)
    key_all = paired_got[0, :, :HEAD_SIZE]
    value_all = paired_got[0, :, HEAD_SIZE:]
    total_rows = units * qcount
    qblock = min(total_rows, 512)
    kblock = min(group, 256)
    key_blocks = group // kblock
    span = (qblock // part_rows - 1) * token_rows + part_rows
    span = min(group, span)
    slots_most = min(key_blocks, (longest + span - 1 + kblock - 1) // kblock + 1)
    scale = HEAD_SIZE ** (-0.5)

    def attend(args):
        qrows, qpoint, qdoc, qpos = args
        last_point = jnp.max(qpoint)
        first_key = jnp.min(qpoint - qpos)
        block_low = first_key // kblock
        block_high = last_point // kblock
        count = jnp.minimum(block_high - block_low + 1, slots_most)

        def score_block(slot, stored):
            index = block_low + slot
            kslice = lax.dynamic_slice_in_dim(key_all, index * kblock, kblock, 0)
            kpoint = index * kblock + jnp.arange(kblock, dtype=jnp.int32)
            kdoc = lax.dynamic_slice_in_dim(key_doc, index * kblock, kblock, 0)
            allowed = (qdoc[:, None] == kdoc[None, :]) & (kpoint[None, :] <= qpoint[:, None])
            scores = (
                jnp.einsum("qd,kd->qk", qrows, kslice, preferred_element_type=jnp.float32) * scale
            )
            scores = jnp.where(allowed, scores, -jnp.inf)
            return lax.dynamic_update_slice_in_dim(stored, scores, slot * kblock, 1)

        stored = jnp.full((qblock, slots_most * kblock), -jnp.inf, jnp.float32)
        stored = lax.fori_loop(0, count, score_block, stored)
        top = jnp.max(stored, axis=1)

        def accumulate(slot, carry):
            total, summed = carry
            scores = lax.dynamic_slice_in_dim(stored, slot * kblock, kblock, 1)
            weights = jnp.exp(scores - top[:, None])
            vslice = lax.dynamic_slice_in_dim(value_all, (block_low + slot) * kblock, kblock, 0)
            summed = summed + jnp.dot(
                weights.astype(jnp.bfloat16), vslice, preferred_element_type=jnp.float32
            )
            return (total + jnp.sum(weights, axis=1), summed)

        start = (jnp.zeros((qblock,), jnp.float32), jnp.zeros((qblock, HEAD_SIZE), jnp.float32))
        total, summed = lax.fori_loop(0, count, accumulate, start)
        return (summed / total[:, None]).astype(jnp.bfloat16)

    blocks = total_rows // qblock
    attended = lax.map(
        attend,
        (
            query_got.reshape(blocks, qblock, HEAD_SIZE),
            query_points.reshape(blocks, qblock),
            query_doc.reshape(blocks, qblock),
            query_pos.reshape(blocks, qblock),
        ),
    )
    attended = attended.reshape(units, qcount, HEAD_SIZE)
    returned = lax.all_to_all(attended, "sp", split_axis=1, concat_axis=0, tiled=True)
    return jnp.transpose(
        returned.reshape(QUERY_HEADS, splits, part_rows, HEAD_SIZE), (1, 2, 0, 3)
    ).reshape(token_rows, QUERY_HEADS * HEAD_SIZE)


def solution(mesh):
    in_specs = (
        P(("dp", "sp"), None),
        P(("dp", "sp"), None),
        P(("dp", "sp")),
        P(("dp", "sp")),
        P("dp", None),
    )
    out_specs = P(("dp", "sp"), None)
    return jax.shard_map(
        on_device, mesh=mesh, in_specs=in_specs, out_specs=out_specs, check_vma=False
    )
```

profile of v0, /device:TPU:1, one launch (start us, length us, event | category | flops | bytes accessed | tf_op | source)
XLA Modules:
  0.0 622.4 jit_solution(9536278594395741496)
XLA Ops:
  14.7 9.0 %all-to-all-start = ((s32[8,1,64]{2,1,0:T(1,128)}), s32[8,1,64]{2,1,0:T(1,128)S(1)}, u32[]{:S(2)}, u32[]{:S(2)}) async-start(s32[8,1,64]{2,1,0:T(1,128)} %all_to_all.15), calls=%async_computation | async-start | bytes 8192 | tf_op jit(solution)/shard_map/all_to_all | solution.py:51
  36.6 48.6 %all-to-all-done.1 = bf16[8,64,2048]{2,1,0:T(8,128)(2,1)S(1)} async-done(((bf16[8,64,2048]{2,1,0:T(8,128)(2,1)}), bf16[8,64,2048]{2,1,0:T(8,128)(2,1)S(1)}, u32[]{:S(2)}, u32[]{:S(2)}) %all-to-all-start.1) | async-done | bytes 2097184 | tf_op jit(solution)/shard_map/all_to_all | solution.py:48
  89.2 57.3 %all-gather.2.cloned.1.call-done = bf16[2048,3072]{1,0:T(8,128)(2,1)} async-done(((bf16[8,3072]{1,0:T(8,128)(2,1)}), bf16[2048,3072]{1,0:T(8,128)(2,1)}) %all-gather.2.cloned.1.call-update) | async-done | bytes 12582928 | tf_op jit(solution)/shard_map/all_gather | solution.py:60
  146.5 8.0 %convolution_convert_fusion = bf16[256,3072]{1,0:T(8,128)(2,1)S(1)} fusion(bf16[256,2048]{1,0:T(8,128)(2,1)S(1)} %scatter_custom_fusion.2, bf16[2048,3072]{1,0:T(8,128)(2,1)} %all-gather.2.cloned.1.call-done), kind=kOutput, calls=%fused_computation.25 | convolution fusion | flops 3222011904 | bytes 15204352 | tf_op jit(solution)/shard_map/dot_general | solution.py:58
  170.3 45.2 %all-to-all-done.3 = bf16[32,256,256]{2,1,0:T(8,128)(2,1)} async-done(((bf16[32,256,256]{2,1,0:T(8,128)(2,1)}), bf16[32,256,256]{2,1,0:T(8,128)(2,1)}, u32[]{:S(2)}, u32[]{:S(2)}) %all-to-all-start.3) | async-done | bytes 4194336 | tf_op jit(solution)/shard_map/all_to_all | solution.py:88
  215.5 7.8 %all-to-all-start.2 = ((bf16[32,128,128]{2,1,0:T(8,128)(2,1)}), bf16[32,128,128]{2,1,0:T(8,128)(2,1)}, u32[]{:S(2)}, u32[]{:S(2)}) async-start(bf16[32,128,128]{2,1,0:T(8,128)(2,1)} %bitcast.19), calls=%async_computation.2 | async-start | bytes 2097152 | tf_op jit(solution)/shard_map/all_to_all | solution.py:87
  227.2 13.4 %all-to-all-done.2 = bf16[32,128,128]{2,1,0:T(8,128)(2,1)} async-done(((bf16[32,128,128]{2,1,0:T(8,128)(2,1)}), bf16[32,128,128]{2,1,0:T(8,128)(2,1)}, u32[]{:S(2)}, u32[]{:S(2)}) %all-to-all-start.2) | async-done | bytes 1048608 | tf_op jit(solution)/shard_map/all_to_all | solution.py:87
  240.6 313.3 %while.65 = (s32[]{:T(128)}, bf16[8,512,128]{2,1,0:T(8,128)(2,1)}, s32[8,512]{1,0:T(8,128)S(1)}, s32[8,512]{1,0:T(8,128)S(1)}, s32[8,512]{1,0:T(8,128)S(1)}, /*i...) while((s32[]{:T(128)}, bf16[8,512,128]{2,1,0:T(8,128)(2,1)}, ...), condition=%wide.region_21.22_spmd, body=%wide.region_12.21_spmd.sunk | while | flops 70190384 | bytes 19051316 | solution.py:154
  251.0 7.9 %while.66 = (s32[]{:T(128)}, f32[512,3328]{0,1:T(8,128)}, s32[]{:T(128)}, s32[512]{0:T(512)S(1)}, s32[]{:T(128)}, /*index=5*/s32[8192]{0:T(1024)S(1)}, s32[512]{...) while((s32[]{:T(128)}, f32[512,3328]{0,1:T(8,128)}, ...), condition=%wide.region_16.16_spmd, body=%wide.region_15.15_spmd.sunk | while | flops 34210056 | bytes 730365 | solution.py:136
  281.0 15.8 %while.66 = (s32[]{:T(128)}, f32[512,3328]{0,1:T(8,128)}, s32[]{:T(128)}, s32[512]{0:T(512)S(1)}, s32[]{:T(128)}, /*index=5*/s32[8192]{0:T(1024)S(1)}, s32[512]{...) while((s32[]{:T(128)}, f32[512,3328]{0,1:T(8,128)}, ...), condition=%wide.region_16.16_spmd, body=%wide.region_15.15_spmd.sunk | while | flops 34210056 | bytes 730365 | solution.py:136
  300.2 15.0 %while.67 = (s32[]{:T(128)}, f32[512]{0:T(512)S(1)}, f32[512,128]{1,0:T(8,128)S(1)}, s32[]{:T(128)}, f32[512,3328]{0,1:T(8,128)}, /*index=5*/f32[512]{0:T(512)S(...) while((s32[]{:T(128)}, f32[512]{0:T(512)S(1)}, ...), condition=%wide.region_20.20_spmd, body=%wide.region_18.19_spmd.sunk | while | flops 34144264 | bytes 3748077 | solution.py:150
  326.4 11.8 %while.66 = (s32[]{:T(128)}, f32[512,3328]{0,1:T(8,128)}, s32[]{:T(128)}, s32[512]{0:T(512)S(1)}, s32[]{:T(128)}, /*index=5*/s32[8192]{0:T(1024)S(1)}, s32[512]{...) while((s32[]{:T(128)}, f32[512,3328]{0,1:T(8,128)}, ...), condition=%wide.region_16.16_spmd, body=%wide.region_15.15_spmd.sunk | while | flops 34210056 | bytes 730365 | solution.py:136
  341.7 11.3 %while.67 = (s32[]{:T(128)}, f32[512]{0:T(512)S(1)}, f32[512,128]{1,0:T(8,128)S(1)}, s32[]{:T(128)}, f32[512,3328]{0,1:T(8,128)}, /*index=5*/f32[512]{0:T(512)S(...) while((s32[]{:T(128)}, f32[512]{0:T(512)S(1)}, ...), condition=%wide.region_20.20_spmd, body=%wide.region_18.19_spmd.sunk | while | flops 34144264 | bytes 3748077 | solution.py:150
  364.1 19.7 %while.66 = (s32[]{:T(128)}, f32[512,3328]{0,1:T(8,128)}, s32[]{:T(128)}, s32[512]{0:T(512)S(1)}, s32[]{:T(128)}, /*index=5*/s32[8192]{0:T(1024)S(1)}, s32[512]{...) while((s32[]{:T(128)}, f32[512,3328]{0,1:T(8,128)}, ...), condition=%wide.region_16.16_spmd, body=%wide.region_15.15_spmd.sunk | while | flops 34210056 | bytes 730365 | solution.py:136
  387.3 18.8 %while.67 = (s32[]{:T(128)}, f32[512]{0:T(512)S(1)}, f32[512,128]{1,0:T(8,128)S(1)}, s32[]{:T(128)}, f32[512,3328]{0,1:T(8,128)}, /*index=5*/f32[512]{0:T(512)S(...) while((s32[]{:T(128)}, f32[512]{0:T(512)S(1)}, ...), condition=%wide.region_20.20_spmd, body=%wide.region_18.19_spmd.sunk | while | flops 34144264 | bytes 3748077 | solution.py:150
  417.2 9.9 %while.66 = (s32[]{:T(128)}, f32[512,3328]{0,1:T(8,128)}, s32[]{:T(128)}, s32[512]{0:T(512)S(1)}, s32[]{:T(128)}, /*index=5*/s32[8192]{0:T(1024)S(1)}, s32[512]{...) while((s32[]{:T(128)}, f32[512,3328]{0,1:T(8,128)}, ...), condition=%wide.region_16.16_spmd, body=%wide.region_15.15_spmd.sunk | while | flops 34210056 | bytes 730365 | solution.py:136
  430.6 9.4 %while.67 = (s32[]{:T(128)}, f32[512]{0:T(512)S(1)}, f32[512,128]{1,0:T(8,128)S(1)}, s32[]{:T(128)}, f32[512,3328]{0,1:T(8,128)}, /*index=5*/f32[512]{0:T(512)S(...) while((s32[]{:T(128)}, f32[512]{0:T(512)S(1)}, ...), condition=%wide.region_20.20_spmd, body=%wide.region_18.19_spmd.sunk | while | flops 34144264 | bytes 3748077 | solution.py:150
  451.1 11.8 %while.66 = (s32[]{:T(128)}, f32[512,3328]{0,1:T(8,128)}, s32[]{:T(128)}, s32[512]{0:T(512)S(1)}, s32[]{:T(128)}, /*index=5*/s32[8192]{0:T(1024)S(1)}, s32[512]{...) while((s32[]{:T(128)}, f32[512,3328]{0,1:T(8,128)}, ...), condition=%wide.region_16.16_spmd, body=%wide.region_15.15_spmd.sunk | while | flops 34210056 | bytes 730365 | solution.py:136
  466.4 11.3 %while.67 = (s32[]{:T(128)}, f32[512]{0:T(512)S(1)}, f32[512,128]{1,0:T(8,128)S(1)}, s32[]{:T(128)}, f32[512,3328]{0,1:T(8,128)}, /*index=5*/f32[512]{0:T(512)S(...) while((s32[]{:T(128)}, f32[512]{0:T(512)S(1)}, ...), condition=%wide.region_20.20_spmd, body=%wide.region_18.19_spmd.sunk | while | flops 34144264 | bytes 3748077 | solution.py:150
  488.9 7.9 %while.66 = (s32[]{:T(128)}, f32[512,3328]{0,1:T(8,128)}, s32[]{:T(128)}, s32[512]{0:T(512)S(1)}, s32[]{:T(128)}, /*index=5*/s32[8192]{0:T(1024)S(1)}, s32[512]{...) while((s32[]{:T(128)}, f32[512,3328]{0,1:T(8,128)}, ...), condition=%wide.region_16.16_spmd, body=%wide.region_15.15_spmd.sunk | while | flops 34210056 | bytes 730365 | solution.py:136
  518.9 15.8 %while.66 = (s32[]{:T(128)}, f32[512,3328]{0,1:T(8,128)}, s32[]{:T(128)}, s32[512]{0:T(512)S(1)}, s32[]{:T(128)}, /*index=5*/s32[8192]{0:T(1024)S(1)}, s32[512]{...) while((s32[]{:T(128)}, f32[512,3328]{0,1:T(8,128)}, ...), condition=%wide.region_16.16_spmd, body=%wide.region_15.15_spmd.sunk | while | flops 34210056 | bytes 730365 | solution.py:136
  538.1 15.0 %while.67 = (s32[]{:T(128)}, f32[512]{0:T(512)S(1)}, f32[512,128]{1,0:T(8,128)S(1)}, s32[]{:T(128)}, f32[512,3328]{0,1:T(8,128)}, /*index=5*/f32[512]{0:T(512)S(...) while((s32[]{:T(128)}, f32[512]{0:T(512)S(1)}, ...), condition=%wide.region_20.20_spmd, body=%wide.region_18.19_spmd.sunk | while | flops 34144264 | bytes 3748077 | solution.py:150
  557.6 22.4 %reduce.9 = bf16[4096,128]{1,0:T(8,128)(2,1)S(1)} reduce(bf16[4096,1,128]{2,1,0:T(2,128)(2,1)S(1)} %bitcast.84, bf16[]{:T(256)} %broadcast.306), dimensions={1}, to_apply=%bitcast.66.reduce_sub_computation | reduce | bytes 2097154
  580.3 32.1 %all_to_all.44 = bf16[32,2,8192]{2,1,0:T(2,128)(2,1)S(1)} all-to-all(bf16[32,2,8192]{2,1,0:T(2,128)(2,1)S(1)} %reshape.323), channel_id=1, replica_groups=mesh['dp'=8,'sp'=32] {'sp'}, dimensions={0} | all-to-all | bytes 2097152 | tf_op jit(solution)/shard_map/all_to_all | solution.py:164
  (542 shorter events, 340.6 us)
Async XLA Ops:
  6.5 140.0 %all-gather.2.cloned.1.call-start = ((), (), s32[]{:S(2)}) async-start(), calls=%async_computation.5 | async-start | bytes 12632064 | tf_op jit(solution)/shard_map/all_gather | solution.py:60
  14.7 15.5 %all-to-all-start = ((s32[8,1,64]{2,1,0:T(1,128)}), s32[8,1,64]{2,1,0:T(1,128)S(1)}, u32[]{:S(2)}, u32[]{:S(2)}) async-start(s32[8,1,64]{2,1,0:T(1,128)} %all_to_all.15), calls=%async_computation | async-start | bytes 8192 | tf_op jit(solution)/shard_map/all_to_all | solution.py:51
  30.2 55.0 %all-to-all-start.1 = ((bf16[8,64,2048]{2,1,0:T(8,128)(2,1)}), bf16[8,64,2048]{2,1,0:T(8,128)(2,1)S(1)}, u32[]{:S(2)}, u32[]{:S(2)}) async-start(bf16[8,64,2048]{2,1,0:T(8,128)(2,1)} %bitcast.14), calls=%async_computation.1 | async-start | bytes 4194304 | tf_op jit(solution)/shard_map/all_to_all | solution.py:48
  154.5 1.2 copy-start
  159.6 55.9 %all-to-all-start.3 = ((bf16[32,256,256]{2,1,0:T(8,128)(2,1)}), bf16[32,256,256]{2,1,0:T(8,128)(2,1)}, u32[]{:S(2)}, u32[]{:S(2)}) async-start(bf16[32,256,256]{2,1,0:T(8,128)(2,1)} %bitcast.82), calls=%async_computation.3 | async-start | bytes 8388608 | tf_op jit(solution)/shard_map/all_to_all | solution.py:88
  215.5 25.1 %all-to-all-start.2 = ((bf16[32,128,128]{2,1,0:T(8,128)(2,1)}), bf16[32,128,128]{2,1,0:T(8,128)(2,1)}, u32[]{:S(2)}, u32[]{:S(2)}) async-start(bf16[32,128,128]{2,1,0:T(8,128)(2,1)} %bitcast.19), calls=%async_computation.2 | async-start | bytes 2097152 | tf_op jit(solution)/shard_map/all_to_all | solution.py:87
Sparse Core Ops, SparseCore 0:
  11.1 135.3 all-gather.1
where the time goes:
time: 634 us; the launch traced here: 622 us
  waiting for transfers between devices  167 us (26%)
  local copies, waits for them, and re-layouts  134 us (21%)
  matrix products  120 us (19%)
  other arithmetic  89 us (14%)
  loops' own time  39.3 us (6%)
  blocking collectives  32.1 us (5%)
  starting transfers between devices  27 us (4%)
  between operations  13.6 us (2%)
    dot_general x51, matrix products, score_block(): jnp.einsum('qd,kd->qk', qrows, kslice, preferred_element_type=jnp.float32)  96.5 us
    dynamic_slice x102, local copies, waits for them, and re-layouts, accumulate(): scores = lax.dynamic_slice_in_dim(stored, slot * kblock, kblock, 1)  65.1 us
    all_gather x1, waiting for transfers between devices, on_device(): lax.all_gather(qkv_weight, ('dp', 'sp'), axis=0, tiled=True)  57.3 us
    all_to_all x1, waiting for transfers between devices, on_device(): lax.all_to_all(buffer.reshape(n_dp, capacity, feats), 'dp', split_axis=0,...  48.6 us
    all_to_all x1, waiting for transfers between devices, on_device(): lax.all_to_all(partner_outbound, 'sp', split_axis=0, concat_axis=1, tiled...  45.2 us
    another operation x1, loops' own time, on_device(): lax.map(attend, (query_got.reshape(blocks, qblock, HEAD_SIZE), query_poin...  36.4 us
    all_to_all x1, blocking collectives, on_device(): lax.all_to_all(attended, 'sp', split_axis=1, concat_axis=0, tiled=True)  32.1 us
    another operation x26, local copies, waits for them, and re-layouts  30.2 us
  transfers between devices with their start and end apart: 5, of which 5 were waited for; matrix products, arithmetic and copies ran while one was open for 4% of the time, Pallas kernels for 0%

commit v1 on v0

v1 whole, which is shorter than its diff:
```python
import jax
import jax.numpy as jnp
from jax import lax
from jax.experimental import pallas as pl
from jax.experimental.pallas import tpu as pltpu
from jax.sharding import PartitionSpec as P

HEAD_SIZE = 128
ROPE_BASE = 500000.0
N_DP = 8
SIDE = 4
CHIPS = SIDE * SIDE
TOK = 256
CHIP_TOK = 2 * TOK
MODEL = 2048
SLOT = TOK // N_DP
QCOLS = 1024
KVCOLS = 256
COLS = QCOLS + 2 * KVCOLS
HALF = COLS // 2
REACH = 4
MESH = pl.DeviceIdType.MESH
F32 = jnp.float32
BF16 = jnp.bfloat16
I32 = jnp.int32


def iota(shape, dim):
    return lax.broadcasted_iota(I32, shape, dim)


class Copies:
    def __init__(self, send, recv):
        self.send, self.recv, self.made = send, recv, []

    def start(self, src, dst, device):
        n = len(self.made)
        copy = pltpu.make_async_remote_copy(
            src_ref=src,
            dst_ref=dst,
            send_sem=self.send.at[n],
            recv_sem=self.recv.at[n],
            device_id=device,
            device_id_type=MESH,
        )
        copy.start()
        self.made.append(copy)
        return copy

    def drain(self):
        for copy in self.made:
            copy.wait_send()


def meet(devices):
    barrier = pltpu.get_barrier_semaphore()
    for device in devices:
        pl.semaphore_signal(barrier, inc=1, device_id=device, device_id_type=MESH)
    pl.semaphore_wait(barrier, len(devices))


N_PROJECT = 1 + 7 + 2 * 7 + 2 * 7 + 2 * (4 + 16) + 1


def project_kernel(
    tokens, w, route, offset, cosine, sine, q_out, kv_out,
    packed, ids, got, got_ids, extra, extra_ids, wsend, wrecv, wbuf, x, send, recv,
):
    z = lax.axis_index("dp")
    sp = lax.axis_index("sp")
    core = lax.rem(sp, 2)
    chip = sp // 2
    cy, cx = chip // SIDE, lax.rem(chip, SIDE)
    partner = (z, sp + 1 - 2 * core)

    def at_z(d):
        return (lax.rem(z + d + N_DP, N_DP), sp)

    def place(dy, dx):
        return lax.rem(cy + dy + SIDE, SIDE) * SIDE + lax.rem(cx + dx + SIDE, SIDE)

    def at_chip(dy, dx):
        return (z, place(dy, dx) * 2 + core)

    def half_of(c):
        cols = lambda base, width: w[:, pl.ds(pl.multiple_of(base + c * width, 128), width)]
        return [
            (0, QCOLS, cols(0, QCOLS)),
            (QCOLS, KVCOLS, cols(2 * QCOLS, KVCOLS)),
            (QCOLS + KVCOLS, KVCOLS, cols(2 * QCOLS + 2 * KVCOLS, KVCOLS)),
        ]

    for base, width, part in half_of(1 - core):
        wsend[:, base : base + width] = part.astype(F32)

    meet(
        [at_z(d) for d in range(1, N_DP)]
        + [partner]
        + [at_chip(0, 1), at_chip(0, -1), at_chip(1, 0), at_chip(-1, 0)]
    )
    copies = Copies(send, recv)

    swap = copies.start(wsend, wrecv, partner)

    group = iota((8, TOK), 0)
    route_row = route[...]
    onehot = route_row == group
    before = (iota((TOK, TOK), 0) < iota((TOK, TOK), 1)).astype(F32).astype(BF16)
    rank = jnp.dot(
        onehot.astype(F32).astype(BF16), before, preferred_element_type=F32
    ).astype(I32)
    dest = jnp.where(rank < SLOT, group * SLOT + rank, N_DP * SLOT + rank - SLOT)
    dest = jnp.sum(jnp.where(onehot, dest, 0), axis=0, keepdims=True)

    swap.wait_recv()
    for base, width, part in half_of(core):
        own = part.astype(F32)
        other = wrecv[:, base : base + width]
        top = jnp.where(core == 0, own, other)
        bottom = jnp.where(core == 0, other, own)
        wbuf[z, chip, :, base : base + width] = jnp.concatenate([top, bottom], axis=0).astype(BF16)
    wz = [copies.start(wbuf.at[z, chip], wbuf.at[z, chip], at_z(d)) for d in range(1, N_DP)]

    for block in range(N_DP + 1):
        pick = (iota((SLOT, TOK), 0) + block * SLOT == dest).astype(F32).astype(BF16)
        packed[block] = jnp.dot(pick, tokens[...], preferred_element_type=F32).astype(BF16)
    extra[z] = packed[N_DP]

    def ring(s):
        out = []
        right, left = lax.rem(z - s + N_DP, N_DP), lax.rem(z + s, N_DP)
        out.append(copies.start(extra.at[right], extra.at[right], at_z(1)))
        if s < 3:
            out.append(copies.start(extra.at[left], extra.at[left], at_z(-1)))
        return out

    tours = [ring(0)]
    tokens_sent = []
    for d in range(1, N_DP):
        to = lax.rem(z + d, N_DP)
        tokens_sent.append(copies.start(packed.at[to], got.at[z], at_z(d)))
    got[z] = packed[z]

    facts = jnp.where(
        group == 0,
        offset[...] - sp * TOK,
        jnp.where(group == 1, route_row, jnp.where(group == 2, 1, 0)),
    ).astype(F32).astype(BF16)
    lane = iota((TOK, TOK), 0) - z * SLOT
    lane_ok = jnp.where((lane >= 0) & (lane < SLOT), lane, -10 * TOK)
    for block in range(N_DP + 1):
        pick = (lane_ok + block * SLOT == dest).astype(F32).astype(BF16)
        found = lax.dot_general(
            facts, pick, (((1,), (1,)), ((), ())), preferred_element_type=F32
        ).astype(I32)
        number = found[1:2] * TOK + found[0:1] + found[2:3]
        ids[block] = jnp.broadcast_to(number, (8, TOK))
    got_ids[z] = ids[z]
    ids_sent = []
    for d in range(1, N_DP):
        to = lax.rem(z + d, N_DP)
        ids_sent.append(copies.start(ids.at[to], got_ids.at[z], at_z(d)))
    extra_ids[z] = ids[N_DP]
    for d in range(1, N_DP):
        ids_sent.append(copies.start(extra_ids.at[z], extra_ids.at[z], at_z(d)))

    for copy in wz:
        copy.wait_recv()

    class Plane:
        def __init__(self, which, first, second):
            self.which, self.first, self.second = which, first, second

        def at(self, a, b):
            return (a * self.first[0] + b * self.second[0], a * self.first[1] + b * self.second[1])

        def send(self, a, b, z0, zn, to):
            ref = wbuf.at[
                pl.ds(z0, zn), place(*self.at(a, b)), :, pl.ds(self.which * HALF, HALF)
            ]
            return copies.start(ref, ref, at_chip(*self.at(*to)))

        def open(self):
            self.near = [self.send(0, 0, 0, 8, (1, 0)), self.send(0, 0, 0, 8, (-1, 0))]
            self.across = {}

        def spread(self, u):
            self.across[u] = [self.send(u, 0, 0, 8, (0, 1)), self.send(u, 0, 0, 8, (0, -1))]

        def forward(self):
            self.near[0].wait_recv()
            self.far = [self.send(-1, 0, 0, 4, (1, 0))]
            self.near[1].wait_recv()
            self.far.append(self.send(1, 0, 4, 4, (-1, 0)))

        def close(self):
            for copy in self.far:
                copy.wait_recv()

        def pass_on(self, u):
            self.across[u][0].wait_recv()
            one = self.send(u, -1, 0, 4, (0, 1))
            self.across[u][1].wait_recv()
            return [one, self.send(u, 1, 4, 4, (0, -1))]

    planes = [Plane(0, (0, 1), (1, 0)), Plane(1, (1, 0), (0, 1))]

    def ring_step(s):
        for copy in tours[-1]:
            copy.wait_recv()
        if s < 4:
            tours.append(ring(s))

    for plane in planes:
        plane.open()
    for plane in planes:
        plane.spread(0)
    for plane in planes:
        plane.forward()
    ring_step(1)
    for plane in planes:
        plane.spread(-1)
        plane.spread(1)
    for plane in planes:
        plane.close()
        plane.spread(2)
    last = []
    for u in (0, -1, 1, 2):
        for plane in planes:
            last.extend(plane.pass_on(u))
        if u == 0:
            ring_step(2)
        if u == -1:
            ring_step(3)
        if u == 1:
            ring_step(4)

    for copy in tokens_sent + ids_sent:
        copy.wait_recv()
    mine = iota((TOK, TOK), 0) + z * TOK + 1
    total = jnp.zeros((8, TOK), I32)
    more = jnp.zeros((8, TOK), I32)
    for source in range(N_DP):
        total += got_ids[source]
        more += extra_ids[source]
    to_place = (total[0:1] == mine).astype(F32).astype(BF16)
    to_place_more = (more[0:1] == mine).astype(F32).astype(BF16)
    own_rows = pl.ds(pl.multiple_of(core * TOK, TOK), TOK)
    for part in range(4):
        cols = slice(part * 512, part * 512 + 512)
        rows = jnp.dot(
            to_place, got[:, :, cols].reshape(TOK, 512), preferred_element_type=F32
        ) + jnp.dot(
            to_place_more, extra[:, :, cols].reshape(TOK, 512), preferred_element_type=F32
        )
        x[own_rows, cols] = rows.astype(BF16)
    shared = copies.start(x.at[own_rows], x.at[own_rows], partner)
    for copy in last:
        copy.wait_recv()
    shared.wait_recv()

    def project(c):
        cols = pl.ds(pl.multiple_of(c * 256, 256), 256)
        weights = wbuf[:, :, :, cols].reshape(MODEL, 256)
        return jnp.dot(x[...], weights, preferred_element_type=F32).astype(BF16)

    def rotated(y):
        parts = []
        for head in range(2):
            v = y[:, head * 128 : head * 128 + 128].astype(F32)
            parts.append((v * cosine[...] + pltpu.roll(v, 64, 1) * sine[...]).astype(BF16))
        return jnp.concatenate(parts, axis=1)

    kv_out[:, 0:256] = rotated(project(4))
    kv_out[:, 256:512] = project(5)

    def query(c, carry):
        q_out[:, pl.ds(pl.multiple_of(c * 256, 256), 256)] = rotated(project(c))
        return carry

    lax.fori_loop(0, 4, query, 0)
    copies.drain()


NEG = -1e30


def attend_kernel(q, kv, lens, out, kvbuf, keep, keep0, top, total, acc, mine, send, recv):
    z = lax.axis_index("dp")
    sp = lax.axis_index("sp")
    core = lax.rem(sp, 2)
    chip = sp // 2
    partner = (z, sp + 1 - 2 * core)

    def at_chip(d):
        return (z, lax.rem(chip + d + CHIPS, CHIPS) * 2 + core)

    meet(
        [at_chip(d) for d in range(1, REACH + 1)]
        + [at_chip(-d) for d in range(1, REACH + 1)]
        + [partner]
    )
    copies = Copies(send, recv)
    blocks = [copies.start(kv, kvbuf.at[d - 1], at_chip(d)) for d in range(1, REACH + 1)]

    row = iota((CHIP_TOK, 128), 0)
    first = jnp.zeros((CHIP_TOK, 128), I32)
    begin = lens[0, 0] * 0
    for e in range(16):
        first = jnp.where(row + chip * CHIP_TOK >= begin, begin, first)
        begin = begin + lens[0, e]
    first = first - chip * CHIP_TOK
    for t in range(4):
        col = iota((CHIP_TOK, 128), 1) + 128 * t
        keep[:, t * 128 : t * 128 + 128] = col - first
        keep0[:, t * 128 : t * 128 + 128] = jnp.where(col <= row, col - first, -1)

    factor = HEAD_SIZE ** (-0.5) * 1.4426950408889634

    def block_step(d, h):
        source = kv if d == 0 else kvbuf.at[d - 1]
        kcols = pl.ds(pl.multiple_of(h // 4 * 128, 128), 128)
        vcols = pl.ds(pl.multiple_of(256 + h // 4 * 128, 128), 128)
        qcols = pl.ds(pl.multiple_of(h * 128, 128), 128)
        for half in range(2):
            rows = slice(half * 256, half * 256 + 256)
            lo, hi = 0, 512
            if d == 0 and half == 0:
                hi = 256
            if d == REACH and half == 1:
                lo = 256
            keys = source[lo:hi, kcols]
            values = source[lo:hi, vcols]
            s = lax.dot_general(
                q[rows, qcols], keys, (((1,), (1,)), ((), ())), preferred_element_type=F32
            )
            seen = keep0[rows, lo:hi] >= 0 if d == 0 else keep[rows, lo:hi] >= 512 * d
            s = jnp.where(seen, s, NEG)
            best = s[:, 0:128]
            for t in range(1, (hi - lo) // 128):
                best = jnp.maximum(best, s[:, t * 128 : t * 128 + 128])
            best = jnp.broadcast_to(jnp.max(best, axis=1, keepdims=True), (256, 128))
            if d > 0:
                old = top[h, rows]
                best = jnp.maximum(old, best)
                alpha = jnp.exp2((old - best) * factor)
            part, weights = None, []
            for t in range((hi - lo) // 128):
                e = jnp.exp2((s[:, t * 128 : t * 128 + 128] - best) * factor)
                part = e if part is None else part + e
                weights.append(e.astype(BF16))
            pv = jnp.dot(jnp.concatenate(weights, axis=1), values, preferred_element_type=F32)
            if d > 0:
                part = total[h, rows] * alpha + part
                pv = acc[h, rows] * alpha + pv
            if d < REACH:
                top[h, rows] = best
                total[h, rows] = part
                acc[h, rows] = pv
            else:
                result = pv / jnp.sum(part, axis=1, keepdims=True)
                mine[rows, qcols] = result.astype(BF16)

    for d in range(REACH + 1):
        if d > 0:
            blocks[d - 1].wait_recv()

        def head(h, carry, d=d):
            block_step(d, h)
            return carry

        lax.fori_loop(0, 8, head, 0)

    own = pl.ds(pl.multiple_of(core * TOK, TOK), TOK)
    other = pl.ds(pl.multiple_of((1 - core) * TOK, TOK), TOK)
    cols = pl.ds(pl.multiple_of(core * QCOLS, QCOLS), QCOLS)
    back = copies.start(mine.at[other], out.at[:, cols], partner)
    out[:, cols] = mine[own]
    back.wait_recv()
    copies.drain()


def on_device(tokens, qkv_weight, route, offset, doc_lengths):
    chip = lax.axis_index("sp") // 2
    lens = doc_lengths
    ends = jnp.cumsum(lens[0])
    points = chip * CHIP_TOK + jnp.arange(CHIP_TOK, dtype=I32)
    starts = ends - lens[0]
    first = jnp.max(jnp.where(points[:, None] >= starts[None, :], starts[None, :], 0), axis=1)
    pos = points - first
    half = HEAD_SIZE // 2
    freq = ROPE_BASE ** (-(jnp.arange(half, dtype=F32) * 2.0 / HEAD_SIZE))
    angle = pos.astype(F32)[:, None] * freq[None, :]
    cosine, sine = jnp.cos(angle), jnp.sin(angle)
    cosine = jnp.concatenate([cosine, cosine], axis=1)
    sine = jnp.concatenate([-sine, sine], axis=1)

    vmem = pl.BlockSpec(memory_space=pltpu.VMEM)
    q, kv = pl.pallas_call(
        project_kernel,
        out_shape=(
            jax.ShapeDtypeStruct((CHIP_TOK, QCOLS), BF16),
            jax.ShapeDtypeStruct((CHIP_TOK, 2 * KVCOLS), BF16),
        ),
        in_specs=[vmem] * 6,
        out_specs=(vmem, vmem),
        scratch_shapes=[
            pltpu.VMEM((N_DP + 1, SLOT, MODEL), BF16),
            pltpu.VMEM((N_DP + 1, 8, TOK), I32),
            pltpu.VMEM((N_DP, SLOT, MODEL), BF16),
            pltpu.VMEM((N_DP, 8, TOK), I32),
            pltpu.VMEM((N_DP, SLOT, MODEL), BF16),
            pltpu.VMEM((N_DP, 8, TOK), I32),
            pltpu.VMEM((8, COLS), F32),
            pltpu.VMEM((8, COLS), F32),
            pltpu.VMEM((N_DP, CHIPS, 16, COLS), BF16),
            pltpu.VMEM((CHIP_TOK, MODEL), BF16),
            pltpu.SemaphoreType.DMA((N_PROJECT,)),
            pltpu.SemaphoreType.DMA((N_PROJECT,)),
        ],
        compiler_params=pltpu.CompilerParams(
            collective_id=0, has_side_effects=True, vmem_limit_bytes=48 * 2**20
        ),
    )(tokens, qkv_weight, route.reshape(1, TOK), offset.reshape(1, TOK), cosine, sine)

    return pl.pallas_call(
        attend_kernel,
        out_shape=jax.ShapeDtypeStruct((TOK, 2 * QCOLS), BF16),
        in_specs=[vmem, vmem, pl.BlockSpec(memory_space=pltpu.SMEM)],
        out_specs=vmem,
        scratch_shapes=[
            pltpu.VMEM((REACH, CHIP_TOK, 2 * KVCOLS), BF16),
            pltpu.VMEM((CHIP_TOK, CHIP_TOK), I32),
            pltpu.VMEM((CHIP_TOK, CHIP_TOK), I32),
            pltpu.VMEM((8, CHIP_TOK, 128), F32),
            pltpu.VMEM((8, CHIP_TOK, 128), F32),
            pltpu.VMEM((8, CHIP_TOK, 128), F32),
            pltpu.VMEM((CHIP_TOK, QCOLS), BF16),
            pltpu.SemaphoreType.DMA((REACH + 1,)),
            pltpu.SemaphoreType.DMA((REACH + 1,)),
        ],
        compiler_params=pltpu.CompilerParams(
            collective_id=1, has_side_effects=True, vmem_limit_bytes=48 * 2**20
        ),
    )(q, kv, lens)


def solution(mesh):
    in_specs = (
        P(("dp", "sp"), None),
        P(("dp", "sp"), None),
        P(("dp", "sp")),
        P(("dp", "sp")),
        P("dp", None),
    )
    out_specs = P(("dp", "sp"), None)
    return jax.shard_map(
        on_device, mesh=mesh, in_specs=in_specs, out_specs=out_specs, check_vma=False
    )
```

time: 634 us -> 140 us (0.22); the launches traced: 622 us -> 140 us
  waiting for transfers between devices: 167 us -> 0 us
  Pallas kernels: 0 us -> 136 us
  local copies, waits for them, and re-layouts: 134 us -> 2.31 us
  matrix products: 120 us -> 0 us
  other arithmetic: 89 us -> 1.5 us
  loops' own time: 39.3 us -> 0 us
  blocking collectives: 32.1 us -> 0 us
  starting transfers between devices: 27 us -> 0 us
  between operations: 13.6 us -> 0.08 us
    pallas_call x0 -> x2, Pallas kernels: none -> 136 us  [the longest x1 70.6 us: on_device(): pl.pallas_call(project_kernel, out_shape=(jax.ShapeDtypeStruct((CHIP_TOK,...]
    dot_general x103 -> x0, matrix products: 120 us -> none  [the longest x51 96.5 us: score_block(): jnp.einsum('qd,kd->qk', qrows, kslice, preferred_element_type=jnp.float32)]
    all_to_all x4 -> x0, waiting for transfers between devices: 109 us -> none  [the longest x1 48.6 us: on_device(): lax.all_to_all(buffer.reshape(n_dp, capacity, feats), 'dp', split_axis=0,...]
    dynamic_slice x161 -> x0, local copies, waits for them, and re-layouts: 69 us -> none  [the longest x102 65.1 us: accumulate(): scores = lax.dynamic_slice_in_dim(stored, slot * kblock, kblock, 1)]
    all_gather x1 -> x0, waiting for transfers between devices: 57.3 us -> none  [on_device(): lax.all_gather(qkv_weight, ('dp', 'sp'), axis=0, tiled=True)]
    another operation x17 -> x0, loops' own time: 39.3 us -> none  [the longest x1 36.4 us: on_device(): lax.map(attend, (query_got.reshape(blocks, qblock, HEAD_SIZE), query_poin...]
    reduce_max x16 -> x1, other arithmetic: 32.6 us -> 0.09 us  [on_device(): jnp.max(jnp.where(points[:, None] >= starts[None, :], starts[None, :], 0)...]
    all_to_all x1 -> x0, blocking collectives: 32.1 us -> none  [on_device(): lax.all_to_all(attended, 'sp', split_axis=1, concat_axis=0, tiled=True)]
  transfers between devices with their start and end apart: 5 -> 0, of which waited for: 5 -> 0; matrix products, arithmetic and copies ran while one was open for 4% -> 0% of each run, Pallas kernels for 0% -> 0%
where the time goes in v1:
time: 140 us
  Pallas kernels  136 us (97%)
  local copies, waits for them, and re-layouts  2.31 us (2%)
  other arithmetic  1.5 us (1%)
    pallas_call x1, Pallas kernels, on_device(): pl.pallas_call(project_kernel, out_shape=(jax.ShapeDtypeStruct((CHIP_TOK,...  70.6 us
    pallas_call x1, Pallas kernels, on_device(): pl.pallas_call(attend_kernel, out_shape=jax.ShapeDtypeStruct((TOK, 2 * QC...  65.1 us

profile of v1, /device:TPU:1, one launch (start us, length us, event | category | flops | bytes accessed | tf_op | source)
XLA Modules:
  0.0 139.6 jit_solution(10658923880145586451)
XLA Ops:
  0.0 0.0 copy-start.4
  0.0 0.7 copy-done.4
  0.7 0.2 reduce-window_clone.1
  0.9 0.1 select_reduce_fusion
  1.0 0.0 copy-start
  1.0 1.0 fusion
  2.0 0.0 copy-start.1
  2.0 0.0 copy-start.3
  2.0 0.2 pad_maximum_fusion
  2.2 0.0 copy-start.2
  2.2 0.0 copy-done
  2.2 0.6 copy-done.1
  2.8 0.0 copy-done.3
  2.8 0.1 copy-done.2
  2.9 70.6 %shard_map.55 = (bf16[512,1024]{1,0:T(8,128)(2,1)S(1)}, bf16[512,512]{1,0:T(8,128)(2,1)S(1)}) custom-call(bf16[256,2048]{1,0:T(8,128)(2,1)S(1)} %copy-done, bf16[8,3072]{1,0:T(8,128)(2,1)S(1)} %copy-done.1, s32[1,256]{1,0:T(1,128)S(1)} %bitcast.4, s32[1,256]{1,0:T(1,128)S(1)} %bitcast.5, f32[512,128]{1,0:T(8,128)S(1)} %get-tuple-element.12.cosine, ...), custom_call_target="tpu_custom_call" | custom-call | tf_op jit(solution)/shard_map/pallas_call | solution.py:399
  73.5 65.1 %shard_map.56 = bf16[256,2048]{1,0:T(8,128)(2,1)S(1)} custom-call(bf16[512,1024]{1,0:T(8,128)(2,1)S(1)} %get-tuple-element.7.q, bf16[512,512]{1,0:T(8,128)(2,1)S(1)} %get-tuple-element.8.kv, s32[1,16]{1,0:T(1,128)S(1)} %copy-done.4), custom_call_target="tpu_custom_call" | custom-call | tf_op jit(solution)/shard_map/pallas_call | solution.py:426
  138.6 1.0 copy.7
  (4 shorter events, 0.0 us)
Async XLA Ops:
  0.0 0.7 copy-start.4
  1.0 1.3 copy-start
  2.0 0.9 copy-start.1
  2.0 0.8 copy-start.3
  2.2 0.7 copy-start.2

commit v2 on v1

v2 whole, which is shorter than its diff:
```python
import jax
import jax.numpy as jnp
from jax import lax
from jax.experimental import pallas as pl
from jax.experimental.pallas import tpu as pltpu
from jax.sharding import PartitionSpec as P

HEAD_SIZE = 128
ROPE_BASE = 500000.0
N_DP = 8
SIDE = 4
CHIPS = SIDE * SIDE
TOK = 256
CHIP_TOK = 2 * TOK
MODEL = 2048
SLOT = TOK // N_DP
QCOLS = 1024
KVCOLS = 256
COLS = QCOLS + 2 * KVCOLS
HALF = COLS // 2
REACH = 4
HEADS_AT_ONCE = 2
DOCS = 16
PIECES = 4
LEGS = 7
BIG = 2.0**100
FACTOR = HEAD_SIZE ** (-0.5) * 1.4426950408889634
EXTRA_RIGHT, EXTRA_LEFT = 3, 4
W_RIGHT, W_LEFT = 3, 4
MESH = pl.DeviceIdType.MESH
F32 = jnp.float32
BF16 = jnp.bfloat16
I32 = jnp.int32


def iota(shape, dim):
    return lax.broadcasted_iota(I32, shape, dim)


class Copies:
    def __init__(self, send, recv):
        self.send, self.recv, self.made = send, recv, []

    def start(self, src, dst, device):
        n = len(self.made)
        copy = pltpu.make_async_remote_copy(
            src_ref=src,
            dst_ref=dst,
            send_sem=self.send.at[n],
            recv_sem=self.recv.at[n],
            device_id=device,
            device_id_type=MESH,
        )
        copy.start()
        self.made.append(copy)
        return copy

    def drain(self):
        for copy in self.made:
            copy.wait_send()


def meet(devices):
    barrier = pltpu.get_barrier_semaphore()
    for device in devices:
        pl.semaphore_signal(barrier, inc=1, device_id=device, device_id_type=MESH)
    pl.semaphore_wait(barrier, len(devices))


N_COPIES = 1 + 7 + 7 + 7 + 7 + 2 * (4 + 16) + 1 + 2


def kernel(
    tokens, w, route, offset, lens, freq, out,
    packed, ids, got, got_ids, extra, wsend, wrecv, wbuf, x,
    cosine, sine, q, kv, kvbuf, qdoc, kdoc, top, total, acc, mine,
    send, recv, leg_send, leg_recv,
):
    z = lax.axis_index("dp")
    sp = lax.axis_index("sp")
    core = lax.rem(sp, 2)
    chip = sp // 2
    cy, cx = chip // SIDE, lax.rem(chip, SIDE)
    partner = (z, sp + 1 - 2 * core)

    def at_z(d):
        return (lax.rem(z + d + N_DP, N_DP), sp)

    def place(dy, dx):
        return lax.rem(cy + dy + SIDE, SIDE) * SIDE + lax.rem(cx + dx + SIDE, SIDE)

    def at_chip(dy, dx):
        return (z, place(dy, dx) * 2 + core)

    def half_of(c):
        cols = lambda base, width: w[:, pl.ds(pl.multiple_of(base + c * width, 128), width)]
        return [
            (0, QCOLS, cols(0, QCOLS)),
            (QCOLS, KVCOLS, cols(2 * QCOLS, KVCOLS)),
            (QCOLS + KVCOLS, KVCOLS, cols(2 * QCOLS + 2 * KVCOLS, KVCOLS)),
        ]

    for base, width, part in half_of(1 - core):
        wsend[:, base : base + width] = part.astype(F32)

    meet(
        [at_z(d) for d in range(1, N_DP)]
        + [partner]
        + [at_chip(0, 1), at_chip(0, -1), at_chip(1, 0), at_chip(-1, 0)]
    )
    copies = Copies(send, recv)

    swap = copies.start(wsend, wrecv, partner)

    group = iota((8, TOK), 0)
    route_row = route[...]
    onehot = route_row == group
    before = (iota((TOK, TOK), 0) < iota((TOK, TOK), 1)).astype(F32).astype(BF16)
    rank = jnp.dot(
        onehot.astype(F32).astype(BF16), before, preferred_element_type=F32
    ).astype(I32)
    dest = jnp.where(rank < SLOT, group * SLOT + rank, N_DP * SLOT + rank - SLOT)
    dest = jnp.sum(jnp.where(onehot, dest, 0), axis=0, keepdims=True)

    def pack(block):
        pick = (iota((SLOT, TOK), 0) + block * SLOT == dest).astype(F32).astype(BF16)
        return jnp.dot(pick, tokens[...], preferred_element_type=F32).astype(BF16)

    def ring(ref, s, right_steps, left_steps):
        sent = []
        right, left = lax.rem(z - s + N_DP, N_DP), lax.rem(z + s, N_DP)
        if s < right_steps:
            sent.append(copies.start(ref(right), ref(right), at_z(1)))
        if s < left_steps:
            sent.append(copies.start(ref(left), ref(left), at_z(-1)))
        return sent

    def extra_ring(s):
        return ring(lambda i: extra.at[i], s, EXTRA_RIGHT, EXTRA_LEFT)

    def w_ring(s):
        return ring(lambda i: wbuf.at[i, chip], s, W_RIGHT, W_LEFT)

    swap.wait_recv()
    for base, width, part in half_of(core):
        own = part.astype(F32)
        other = wrecv[:, base : base + width]
        first = jnp.where(core == 0, own, other)
        second = jnp.where(core == 0, other, own)
        wbuf[z, chip, :, base : base + width] = jnp.concatenate([first, second], axis=0).astype(BF16)
    w_tour = w_ring(0)

    facts = jnp.where(
        group == 0,
        offset[...] - sp * TOK,
        jnp.where(group == 1, route_row, jnp.where(group == 2, 1, 0)),
    ).astype(F32).astype(BF16)
    lane = iota((TOK, TOK), 0) - z * SLOT
    lane_ok = jnp.where((lane >= 0) & (lane < SLOT), lane, -10 * TOK)

    def numbers_of(block):
        pick = (lane_ok + block * SLOT == dest).astype(F32).astype(BF16)
        found = lax.dot_general(
            facts, pick, (((1,), (1,)), ((), ())), preferred_element_type=F32
        ).astype(I32)
        number = found[1:2] * TOK + found[0:1] + found[2:3]
        return [number[:, 0:128], number[:, 128:256]]

    extra[z] = pack(N_DP)
    more = numbers_of(N_DP) + [jnp.zeros((4, 128), I32)]

    def prepare(d):
        to = lax.rem(z + d, N_DP)
        packed[to] = pack(to)
        ids[to] = jnp.concatenate(numbers_of(to) + more, axis=0)

    def w_step(s):
        for copy in w_tour:
            copy.wait_recv()
        return w_ring(s)

    prepare(4)
    w_tour = w_step(1)
    prepare(3)
    prepare(5)
    w_tour = w_step(2)
    prepare(2)
    prepare(6)
    w_tour = w_step(3)
    prepare(1)
    prepare(7)
    w_tour = w_step(4)

    tokens_sent = []

    def send_tokens(d):
        to = lax.rem(z + d, N_DP)
        tokens_sent.append(copies.start(packed.at[to], got.at[z], at_z(d)))
        tokens_sent.append(copies.start(ids.at[to], got_ids.at[z], at_z(d)))

    def extra_step(s):
        for copy in tour:
            copy.wait_recv()
        return extra_ring(s)

    tour = extra_ring(0)
    send_tokens(4)

    class Plane:
        def __init__(self, which, first, second):
            self.which, self.first, self.second = which, first, second

        def at(self, a, b):
            return (a * self.first[0] + b * self.second[0], a * self.first[1] + b * self.second[1])

        def send(self, a, b, z0, zn, to):
            ref = wbuf.at[
                pl.ds(z0, zn), place(*self.at(a, b)), :, pl.ds(self.which * HALF, HALF)
            ]
            return copies.start(ref, ref, at_chip(*self.at(*to)))

        def open(self):
            self.near = [self.send(0, 0, 0, 8, (1, 0)), self.send(0, 0, 0, 8, (-1, 0))]
            self.across = {}

        def spread(self, u):
            self.across[u] = [self.send(u, 0, 0, 8, (0, 1)), self.send(u, 0, 0, 8, (0, -1))]

        def forward(self):
            self.near[0].wait_recv()
            self.far = [self.send(-1, 0, 0, 4, (1, 0))]
            self.near[1].wait_recv()
            self.far.append(self.send(1, 0, 4, 4, (-1, 0)))

        def close(self):
            for copy in self.far:
                copy.wait_recv()

        def pass_on(self, u):
            self.across[u][0].wait_recv()
            one = self.send(u, -1, 0, 4, (0, 1))
            self.across[u][1].wait_recv()
            return [one, self.send(u, 1, 4, 4, (0, -1))]

    planes = [Plane(0, (0, 1), (1, 0)), Plane(1, (1, 0), (0, 1))]
    for plane in planes:
        plane.open()
    for plane in planes:
        plane.spread(0)

    prepare(0)
    got[z] = packed[z]
    got_ids[z] = ids[z]
    tour = extra_step(1)
    send_tokens(3)
    send_tokens(5)
    for plane in planes:
        plane.forward()
    for plane in planes:
        plane.spread(-1)
        plane.spread(1)

    tour = extra_step(2)
    send_tokens(2)
    send_tokens(6)

    lanes = iota((1, 128), 1)
    starts = jnp.full((1, 128), 2**30, I32)
    ends = jnp.full((1, 128), 2**30, I32)
    row = iota((CHIP_TOK, 128), 0) + chip * CHIP_TOK
    begin_of = jnp.zeros((CHIP_TOK, 128), I32)
    begin = lens[0, 0] * 0
    for e in range(DOCS):
        starts = jnp.where(lanes == e, begin, starts)
        begin_of = jnp.where(row >= begin, begin, begin_of)
        begin = begin + lens[0, e]
        ends = jnp.where(lanes == e, begin, ends)
    angle = (row - begin_of).astype(F32) * freq[...]
    cosine[...] = jnp.cos(angle)
    sine[...] = jnp.sin(angle) * jnp.where(lanes < 64, -1.0, 1.0)

    def member(base):
        point = iota((CHIP_TOK, 128), 0) + base
        return (point >= starts) & (point < ends)

    qdoc[...] = jnp.where(member(chip * CHIP_TOK), 1.0, 0.0).astype(BF16)
    for d in range(REACH + 1):
        kdoc[d] = jnp.where(member((chip - d) * CHIP_TOK), 0.0, -BIG).astype(BF16)

    for plane in planes:
        plane.close()
        plane.spread(2)
    last = []

    def pass_on(u):
        for plane in planes:
            last.extend(plane.pass_on(u))

    pass_on(0)
    tour = extra_step(3)
    send_tokens(1)
    send_tokens(7)
    pass_on(-1)
    pass_on(1)
    tour = extra_step(4)
    pass_on(2)

    for copy in tokens_sent:
        copy.wait_recv()
    mine_ids = iota((TOK, TOK), 0) + z * TOK + 1
    numbers = jnp.zeros((8, 128), I32)
    for source in range(N_DP):
        numbers += got_ids[source]
    to_place = [
        (jnp.concatenate([numbers[n : n + 1], numbers[n + 1 : n + 2]], axis=1) == mine_ids)
        .astype(F32)
        .astype(BF16)
        for n in (0, 2)
    ]
    own_rows = pl.ds(pl.multiple_of(core * TOK, TOK), TOK)
    other_rows = pl.ds(pl.multiple_of((1 - core) * TOK, TOK), TOK)
    for part in range(4):
        cols = slice(part * 512, part * 512 + 512)
        rows = jnp.dot(
            to_place[0], got[:, :, cols].reshape(TOK, 512), preferred_element_type=F32
        ) + jnp.dot(
            to_place[1], extra[:, :, cols].reshape(TOK, 512), preferred_element_type=F32
        )
        x[own_rows, cols] = rows.astype(BF16)
    shared = copies.start(x.at[own_rows], x.at[own_rows], partner)
    for copy in last:
        copy.wait_recv()

    def project(c, rows):
        cols = pl.ds(pl.multiple_of(c * 256, 256), 256)
        weights = wbuf[:, :, :, cols].reshape(MODEL, 256)
        return jnp.dot(x[rows], weights, preferred_element_type=F32).astype(BF16)

    def rotated(y, rows):
        parts = []
        for n in range(2):
            v = y[:, n * 128 : n * 128 + 128].astype(F32)
            parts.append((v * cosine[rows] + pltpu.roll(v, 64, 1) * sine[rows]).astype(BF16))
        return parts

    def project_keys(rows, base):
        keys = rotated(project(4, rows), rows)
        values = project(5, rows).astype(F32)
        for g in range(2):
            kv[2 * g, rows] = keys[g]
            for t in range(2):
                block = values[t * 128 : t * 128 + 128, g * 128 : g * 128 + 128]
                at = pl.ds(pl.multiple_of(base + t * 128, 128), 128)
                kv[2 * g + 1, at] = block.T.astype(BF16)

    project_keys(own_rows, core * TOK)
    shared.wait_recv()
    project_keys(other_rows, (1 - core) * TOK)

    def leg(n, number, d, to, source, when):
        copy = pltpu.make_async_remote_copy(
            src_ref=source,
            dst_ref=kvbuf.at[d - 1, n],
            send_sem=leg_send.at[n, number],
            recv_sem=leg_recv.at[n, d - 1],
            device_id=to,
            device_id_type=MESH,
        )
        return copy, when

    def legs(n):
        own, came = kv.at[n], lambda d: kvbuf.at[d - 1, n]
        inner = (cx == 1) | (cx == 2)
        return [
            leg(n, 0, 4, at_chip(1, 0), own, None),
            leg(n, 1, 1, at_chip(0, 1), own, cx < 3),
            leg(n, 2, 3, at_chip(0, -1), own, cx == 0),
            leg(n, 3, 3, at_chip(0, -1), came(4), cx > 0),
            leg(n, 4, 1, at_chip(0, 1), came(4), cx == 3),
            leg(n, 5, 2, at_chip(0, 1), came(1), inner),
            leg(n, 6, 2, at_chip(0, -1), came(3), inner),
        ]

    routes = [legs(n) for n in range(PIECES)]

    def do(action, n, number):
        copy, when = routes[n][number]
        run = copy.start if action == "start" else copy.wait_send
        if when is None:
            run()
        else:
            pl.when(when)(run)

    def arrived(n, d):
        pltpu.make_async_remote_copy(
            src_ref=kvbuf.at[d - 1, n],
            dst_ref=kvbuf.at[d - 1, n],
            send_sem=leg_send.at[n, 0],
            recv_sem=leg_recv.at[n, d - 1],
            device_id=partner,
            device_id_type=MESH,
        ).wait_recv()
        for number in {4: (3, 4), 1: (5,), 3: (6,), 2: ()}[d]:
            do("start", n, number)

    for n in range(PIECES):
        for number in range(3):
            do("start", n, number)

    def query(c, carry):
        for n, part in enumerate(rotated(project(c, slice(0, CHIP_TOK)), slice(0, CHIP_TOK))):
            q[:, pl.ds(pl.multiple_of(c * 256 + n * 128, 128), 128)] = part
        return carry

    lax.fori_loop(0, 4, query, 0)

    def block_step(d, g, heads, first, last):
        keys_of = kv.at[2 * g] if d == 0 else kvbuf.at[d - 1, 2 * g]
        values_of = kv.at[2 * g + 1] if d == 0 else kvbuf.at[d - 1, 2 * g + 1]
        chains = []
        for r in heads:
            h = g * 4 + r
            qcols = pl.ds(pl.multiple_of(h * 128, 128), 128)
            for half in range(2):
                lo, hi = 0, 512
                if d == 0 and half == 0:
                    hi = 256
                if d == REACH and half == 1:
                    lo = 256
                chains.append((h, qcols, slice(half * 256, half * 256 + 256), half, lo, hi))
        scores, old = [], []
        for h, qcols, qs, half, lo, hi in chains:
            keys = jnp.concatenate([keys_of[lo:hi], kdoc[d, lo:hi]], axis=1)
            query = jnp.concatenate([q[qs, qcols], qdoc[qs]], axis=1)
            s = lax.dot_general(
                keys, query, (((1,), (1,)), ((), ())), preferred_element_type=F32
            )
            if d == 0:
                n = hi - lo
                seen = iota((n, 256), 0) + lo <= iota((n, 256), 1) + half * 256
                s = jnp.where(seen, s, -BIG)
            scores.append(s)
            if not first:
                old.append((top[h, :, qs], total[h, :, qs], acc[h, :, qs]))
        new = []
        for n, (h, qcols, qs, half, lo, hi) in enumerate(chains):
            s = scores[n]
            best = jnp.max(s, axis=0, keepdims=True)
            if not first:
                best = jnp.maximum(old[n][0], best)
                alpha = jnp.exp2((old[n][0] - best) * FACTOR)
            e = jnp.exp2((s - best) * FACTOR)
            part = jnp.sum(e, axis=0, keepdims=True)
            values = jnp.concatenate(
                [values_of[t : t + 128] for t in range(lo, hi, 128)], axis=1
            )
            pv = jnp.dot(values, e.astype(BF16), preferred_element_type=F32)
            if not first:
                part = old[n][1] * alpha + part
                pv = old[n][2] * alpha + pv
            new.append((best, part, pv))
        for (best, part, pv), (h, qcols, qs, half, lo, hi) in zip(new, chains):
            if last:
                mine[qs, qcols] = (pv / part).T.astype(BF16)
            else:
                top[h, :, qs] = best
                total[h, :, qs] = part
                acc[h, :, qs] = pv

    def attend(d, g, first=False, last=False):
        def heads(r, carry):
            block_step(d, g, [r * HEADS_AT_ONCE + n for n in range(HEADS_AT_ONCE)], first, last)
            return carry

        lax.fori_loop(0, 4 // HEADS_AT_ONCE, heads, 0)

    out_cols = lambda g: pl.ds(pl.multiple_of(core * QCOLS + g * 512, 512), 512)

    def give(g):
        cols = slice(g * 512, g * 512 + 512)
        return copies.start(mine.at[other_rows, cols], out.at[:, out_cols(g)], partner)

    for n, d in ((0, 4), (0, 1)):
        arrived(n, d)
    attend(0, 0, first=True)
    for n, d in ((1, 4), (1, 1), (0, 3)):
        arrived(n, d)
    attend(0, 1, first=True)
    for n, d in ((2, 4), (2, 1), (1, 3)):
        arrived(n, d)
    attend(4, 0)
    for n, d in ((3, 4), (3, 1), (2, 3)):
        arrived(n, d)
    attend(1, 0)
    arrived(3, 3)
    attend(4, 1)
    attend(1, 1)
    attend(3, 0)
    attend(3, 1)
    arrived(0, 2)
    arrived(1, 2)
    attend(2, 0, last=True)
    back = [give(0)]
    arrived(2, 2)
    arrived(3, 2)
    attend(2, 1, last=True)
    back.append(give(1))
    for g in range(2):
        out[:, out_cols(g)] = mine[own_rows, g * 512 : g * 512 + 512]
    for copy in back:
        copy.wait_recv()
    copies.drain()
    for n in range(PIECES):
        for number in range(LEGS):
            do("wait", n, number)


def on_device(tokens, qkv_weight, route, offset, doc_lengths):
    half = HEAD_SIZE // 2
    freq = ROPE_BASE ** (-(jnp.arange(half, dtype=F32) * 2.0 / HEAD_SIZE))
    freq = jnp.concatenate([freq, freq])[None]
    vmem = pl.BlockSpec(memory_space=pltpu.VMEM)
    smem = pl.BlockSpec(memory_space=pltpu.SMEM)
    return pl.pallas_call(
        kernel,
        out_shape=jax.ShapeDtypeStruct((TOK, 2 * QCOLS), BF16),
        in_specs=[vmem, vmem, vmem, vmem, smem, vmem],
        out_specs=vmem,
        scratch_shapes=[
            pltpu.VMEM((N_DP, SLOT, MODEL), BF16),
            pltpu.VMEM((N_DP, 8, 128), I32),
            pltpu.VMEM((N_DP, SLOT, MODEL), BF16),
            pltpu.VMEM((N_DP, 8, 128), I32),
            pltpu.VMEM((N_DP, SLOT, MODEL), BF16),
            pltpu.VMEM((8, COLS), F32),
            pltpu.VMEM((8, COLS), F32),
            pltpu.VMEM((N_DP, CHIPS, 16, COLS), BF16),
            pltpu.VMEM((CHIP_TOK, MODEL), BF16),
            pltpu.VMEM((CHIP_TOK, HEAD_SIZE), F32),
            pltpu.VMEM((CHIP_TOK, HEAD_SIZE), F32),
            pltpu.VMEM((CHIP_TOK, QCOLS), BF16),
            pltpu.VMEM((PIECES, CHIP_TOK, HEAD_SIZE), BF16),
            pltpu.VMEM((REACH, PIECES, CHIP_TOK, HEAD_SIZE), BF16),
            pltpu.VMEM((CHIP_TOK, 128), BF16),
            pltpu.VMEM((REACH + 1, CHIP_TOK, 128), BF16),
            pltpu.VMEM((8, 1, CHIP_TOK), F32),
            pltpu.VMEM((8, 1, CHIP_TOK), F32),
            pltpu.VMEM((8, HEAD_SIZE, CHIP_TOK), F32),
            pltpu.VMEM((CHIP_TOK, QCOLS), BF16),
            pltpu.SemaphoreType.DMA((N_COPIES,)),
            pltpu.SemaphoreType.DMA((N_COPIES,)),
            pltpu.SemaphoreType.DMA((PIECES, LEGS)),
            pltpu.SemaphoreType.DMA((PIECES, REACH)),
        ],
        compiler_params=pltpu.CompilerParams(
            collective_id=0, has_side_effects=True, vmem_limit_bytes=50 * 2**20
        ),
    )(tokens, qkv_weight, route.reshape(1, TOK), offset.reshape(1, TOK), doc_lengths, freq)


def solution(mesh):
    in_specs = (
        P(("dp", "sp"), None),
        P(("dp", "sp"), None),
        P(("dp", "sp")),
        P(("dp", "sp")),
        P("dp", None),
    )
    out_specs = P(("dp", "sp"), None)
    return jax.shard_map(
        on_device, mesh=mesh, in_specs=in_specs, out_specs=out_specs, check_vma=False
    )
```

time: 140 us -> 109 us (0.78)
  Pallas kernels: 136 us -> 105 us
  other arithmetic: 1.5 us -> 0.09 us
    pallas_call x2 -> x1, Pallas kernels: 136 us -> 105 us  [on_device(): pl.pallas_call(kernel, out_shape=jax.ShapeDtypeStruct((TOK, 2 * QCOLS), B...]
where the time goes in v2:
time: 109 us
  Pallas kernels  105 us (96%)
  local copies, waits for them, and re-layouts  3.59 us (3%)
    pallas_call x1, Pallas kernels, on_device(): pl.pallas_call(kernel, out_shape=jax.ShapeDtypeStruct((TOK, 2 * QCOLS), B...  105 us
    unnamed x11, local copies, waits for them, and re-layouts  3.59 us

profile of v2, /device:TPU:1, one launch (start us, length us, event | category | flops | bytes accessed | tf_op | source)
XLA Modules:
  0.0 109.1 jit_solution(2124650827102903207)
XLA Ops:
  0.0 0.0 copy-start.3
  0.0 0.0 copy-start.2
  0.0 0.0 copy-start.4
  0.0 0.1 maximum_bitcast_fusion.freq
  0.1 0.6 copy-done.3
  0.7 0.0 copy-done.2
  0.7 0.0 copy-done.4
  0.7 0.0 copy-start
  0.7 1.2 %copy-done = bf16[256,2048]{1,0:T(8,128)(2,1)S(1)} copy-done((bf16[256,2048]{1,0:T(8,128)(2,1)S(1)}, bf16[256,2048]{1,0:T(8,128)(2,1)}, u32[]{:S(2)}) %copy-start) | copy-done | bytes 1048600
  1.9 0.0 copy-start.1
  1.9 0.8 copy-done.1
  2.7 105.4 %shard_map.55 = bf16[256,2048]{1,0:T(8,128)(2,1)S(1)} custom-call(bf16[256,2048]{1,0:T(8,128)(2,1)S(1)} %copy-done, bf16[8,3072]{1,0:T(8,128)(2,1)S(1)} %copy-done.1, s32[1,256]{1,0:T(1,128)S(1)} %bitcast.4, s32[1,256]{1,0:T(1,128)S(1)} %bitcast.5, s32[1,16]{1,0:T(1,128)S(1)} %copy-done.4, f32[1,128]{1,0:T(1,128)S(1)} %maximum_bitcast_fusion.freq), custom_call_target="tpu_custom_call" | custom-call | tf_op jit(solution)/shard_map/pallas_call | solution.py:524
  108.1 1.0 copy.7
  (1 shorter events, 0.0 us)
Async XLA Ops:
  0.0 0.7 copy-start.3
  0.0 0.7 copy-start.2
  0.0 0.7 copy-start.4
  0.7 1.2 %copy-start = (bf16[256,2048]{1,0:T(8,128)(2,1)S(1)}, bf16[256,2048]{1,0:T(8,128)(2,1)}, u32[]{:S(2)}) copy-start(bf16[256,2048]{1,0:T(8,128)(2,1)} %tokens.1) | copy-start | bytes 3145732
  1.9 0.8 copy-start.1

commit v3 on v2

--- a/solution.py
+++ b/solution.py
@@ -22,11 +22,26 @@
 HEADS_AT_ONCE = 2
 DOCS = 16
 PIECES = 4
-LEGS = 7
+LEGS = 12
+PASSING = 5
 BIG = 2.0**100
 FACTOR = HEAD_SIZE ** (-0.5) * 1.4426950408889634
-EXTRA_RIGHT, EXTRA_LEFT = 3, 4
+EXTRA_RIGHT, EXTRA_LEFT = 4, 3
 W_RIGHT, W_LEFT = 3, 4
+ORDER = ((0, 0), (0, 1), (4, 0), (1, 0), (4, 1), (1, 1), (3, 0), (3, 1), (2, 0), (2, 1))
+ARRIVALS = (
+    ((), (), (), ()),
+    ((), (), (), ()),
+    (((0, 4), (2, 5), (1, 4), (3, 5),), ((0, 1), (0, 4), (1, 1), (1, 4),), ((0, 1), (0, 4), (1, 1), (1, 4),), ((0, 3), (0, 1), (0, 4), (1, 3), (1, 1), (1, 4),)),
+    (((2, 4), (0, 3), (0, 1), (3, 4), (1, 3), (1, 1),), (), (), ()),
+    (((2, 3),), ((2, 1), (2, 4), (0, 3), (3, 1), (3, 4),), ((2, 1), (2, 4), (0, 3), (3, 1), (3, 4),), ((2, 3), (2, 1), (2, 4), (3, 3), (3, 1), (3, 4),)),
+    (((0, 2), (2, 1), (3, 3), (1, 2), (3, 1),), ((1, 3),), ((1, 3),), ()),
+    ((), ((2, 3),), ((0, 2), (2, 2),), ((0, 2), (2, 2), (2, 5),)),
+    (((2, 2),), ((0, 2), (3, 3),), ((1, 2), (2, 3), (3, 2), (3, 3),), ((1, 2), (3, 2), (3, 5),)),
+    (((3, 2),), ((2, 2), (1, 2),), (), ()),
+    ((), ((3, 2),), (), ()),
+    ((), (), (), ()),
+)
 MESH = pl.DeviceIdType.MESH
 F32 = jnp.float32
 BF16 = jnp.bfloat16
@@ -60,21 +75,22 @@
             copy.wait_send()
 
 
-def meet(devices):
+def greet(devices):
     barrier = pltpu.get_barrier_semaphore()
     for device in devices:
         pl.semaphore_signal(barrier, inc=1, device_id=device, device_id_type=MESH)
-    pl.semaphore_wait(barrier, len(devices))
-
-
-N_COPIES = 1 + 7 + 7 + 7 + 7 + 2 * (4 + 16) + 1 + 2
+    return lambda: pl.semaphore_wait(barrier, len(devices))
+
+
+N_COPIES = 1 + 7 + 7 + 2 * 7 + 2 * 2 * (4 + 16) + 4 + 2
 
 
 def kernel(
-    tokens, w, route, offset, lens, freq, out,
+    tokens_in, w_in, route_in, offset_in, lens, freq, out,
+    tokens, w, route, offset,
     packed, ids, got, got_ids, extra, wsend, wrecv, wbuf, x,
     cosine, sine, q, kv, kvbuf, qdoc, kdoc, top, total, acc, mine,
-    send, recv, leg_send, leg_recv,
+    send, recv, leg_send, leg_recv, load,
 ):
     z = lax.axis_index("dp")
     sp = lax.axis_index("sp")
@@ -100,17 +116,30 @@
             (QCOLS + KVCOLS, KVCOLS, cols(2 * QCOLS + 2 * KVCOLS, KVCOLS)),
         ]
 
-    for base, width, part in half_of(1 - core):
-        wsend[:, base : base + width] = part.astype(F32)
-
-    meet(
+    met = greet(
         [at_z(d) for d in range(1, N_DP)]
         + [partner]
         + [at_chip(0, 1), at_chip(0, -1), at_chip(1, 0), at_chip(-1, 0)]
     )
+    loads = [
+        pltpu.make_async_copy(here, there, load.at[n])
+        for n, (here, there) in enumerate(
+            [(w_in, w), (route_in, route), (offset_in, offset), (tokens_in, tokens)]
+        )
+    ]
+    for copy in loads:
+        copy.start()
+    loads[0].wait()
+    for base, width, part in half_of(1 - core):
+        wsend[:, base : base + width] = part.astype(F32)
+
+    met()
     copies = Copies(send, recv)
 
     swap = copies.start(wsend, wrecv, partner)
+
+    for copy in loads[1:]:
+        copy.wait()
 
     group = iota((8, TOK), 0)
     route_row = route[...]
@@ -126,20 +155,23 @@
         pick = (iota((SLOT, TOK), 0) + block * SLOT == dest).astype(F32).astype(BF16)
         return jnp.dot(pick, tokens[...], preferred_element_type=F32).astype(BF16)
 
-    def ring(ref, s, right_steps, left_steps):
+    def extra_ring(s):
         sent = []
         right, left = lax.rem(z - s + N_DP, N_DP), lax.rem(z + s, N_DP)
-        if s < right_steps:
-            sent.append(copies.start(ref(right), ref(right), at_z(1)))
-        if s < left_steps:
-            sent.append(copies.start(ref(left), ref(left), at_z(-1)))
+        if s < EXTRA_RIGHT:
+            sent.append(copies.start(extra.at[right], extra.at[right], at_z(1)))
+        if s < EXTRA_LEFT:
+            sent.append(copies.start(extra.at[left], extra.at[left], at_z(-1)))
         return sent
 
-    def extra_ring(s):
-        return ring(lambda i: extra.at[i], s, EXTRA_RIGHT, EXTRA_LEFT)
-
     def w_ring(s):
-        return ring(lambda i: wbuf.at[i, chip], s, W_RIGHT, W_LEFT)
+        sent = []
+        if s < W_RIGHT:
+            here, there = (1 - s) % N_DP, -s % N_DP
+            sent.append(copies.start(wbuf.at[here, chip], wbuf.at[there, chip], at_z(1)))
+        if s < W_LEFT:
+            sent.append(copies.start(wbuf.at[1 + s, chip], wbuf.at[2 + s, chip], at_z(-1)))
+        return sent
 
     swap.wait_recv()
     for base, width, part in half_of(core):
@@ -147,7 +179,7 @@
         other = wrecv[:, base : base + width]
         first = jnp.where(core == 0, own, other)
         second = jnp.where(core == 0, other, own)
-        wbuf[z, chip, :, base : base + width] = jnp.concatenate([first, second], axis=0).astype(BF16)
+        wbuf[1, chip, :, base : base + width] = jnp.concatenate([first, second], axis=0).astype(BF16)
     w_tour = w_ring(0)
 
     facts = jnp.where(
@@ -179,18 +211,6 @@
             copy.wait_recv()
         return w_ring(s)
 
-    prepare(4)
-    w_tour = w_step(1)
-    prepare(3)
-    prepare(5)
-    w_tour = w_step(2)
-    prepare(2)
-    prepare(6)
-    w_tour = w_step(3)
-    prepare(1)
-    prepare(7)
-    w_tour = w_step(4)
-
     tokens_sent = []
 
     def send_tokens(d):
@@ -203,34 +223,32 @@
             copy.wait_recv()
         return extra_ring(s)
 
-    tour = extra_ring(0)
-    send_tokens(4)
-
     class Plane:
-        def __init__(self, which, first, second):
+        def __init__(self, which, first, second, low, middle, high):
             self.which, self.first, self.second = which, first, second
+            self.all, self.one, self.two = (low, high), (low, middle), (middle, high)
 
         def at(self, a, b):
             return (a * self.first[0] + b * self.second[0], a * self.first[1] + b * self.second[1])
 
-        def send(self, a, b, z0, zn, to):
+        def send(self, a, b, blocks, to):
             ref = wbuf.at[
-                pl.ds(z0, zn), place(*self.at(a, b)), :, pl.ds(self.which * HALF, HALF)
+                pl.ds(blocks[0], blocks[1] - blocks[0]), place(*self.at(a, b)), :, pl.ds(self.which * HALF, HALF)
             ]
             return copies.start(ref, ref, at_chip(*self.at(*to)))
 
         def open(self):
-            self.near = [self.send(0, 0, 0, 8, (1, 0)), self.send(0, 0, 0, 8, (-1, 0))]
+            self.near = [self.send(0, 0, self.all, (1, 0)), self.send(0, 0, self.all, (-1, 0))]
             self.across = {}
 
         def spread(self, u):
-            self.across[u] = [self.send(u, 0, 0, 8, (0, 1)), self.send(u, 0, 0, 8, (0, -1))]
+            self.across[u] = [self.send(u, 0, self.all, (0, 1)), self.send(u, 0, self.all, (0, -1))]
 
         def forward(self):
             self.near[0].wait_recv()
-            self.far = [self.send(-1, 0, 0, 4, (1, 0))]
+            self.far = [self.send(-1, 0, self.one, (1, 0))]
             self.near[1].wait_recv()
-            self.far.append(self.send(1, 0, 4, 4, (-1, 0)))
+            self.far.append(self.send(1, 0, self.two, (-1, 0)))
 
         def close(self):
             for copy in self.far:
@@ -238,31 +256,69 @@
 
         def pass_on(self, u):
             self.across[u][0].wait_recv()
-            one = self.send(u, -1, 0, 4, (0, 1))
+            one = self.send(u, -1, self.one, (0, 1))
             self.across[u][1].wait_recv()
-            return [one, self.send(u, 1, 4, 4, (0, -1))]
-
-    planes = [Plane(0, (0, 1), (1, 0)), Plane(1, (1, 0), (0, 1))]
-    for plane in planes:
-        plane.open()
-    for plane in planes:
-        plane.spread(0)
-
+            return [one, self.send(u, 1, self.two, (0, -1))]
+
+    near, rest = (
+        [Plane(0, (0, 1), (1, 0), *blocks), Plane(1, (1, 0), (0, 1), *blocks)]
+        for blocks in ((0, 2, 3), (3, 5, 8))
+    )
+    last = []
+
+    def open_plane(planes):
+        for plane in planes:
+            plane.open()
+        for plane in planes:
+            plane.spread(0)
+
+    def widen(planes):
+        for plane in planes:
+            plane.forward()
+        for plane in planes:
+            plane.spread(-1)
+            plane.spread(1)
+
+    def finish(planes):
+        for plane in planes:
+            plane.close()
+            plane.spread(2)
+
+    def pass_on(planes, u):
+        for plane in planes:
+            last.extend(plane.pass_on(u))
+
+    tour = extra_ring(0)
+    for d in (1, 7):
+        prepare(d)
+        send_tokens(d)
+    w_tour = w_step(1)
+    open_plane(near)
+    for d in (3, 2):
+        prepare(d)
+    tour = extra_step(1)
+    widen(near)
+    w_tour = w_step(2)
+    tour = extra_step(2)
+    send_tokens(3)
+    for d in (5, 6, 4):
+        prepare(d)
+    finish(near)
+    pass_on(near, 0)
+    w_tour = w_step(3)
+    send_tokens(5)
+    send_tokens(2)
+    pass_on(near, -1)
+    tour = extra_step(3)
+    send_tokens(6)
+    send_tokens(4)
+    pass_on(near, 1)
+    w_tour = w_step(4)
+    open_plane(rest)
+    pass_on(near, 2)
     prepare(0)
     got[z] = packed[z]
     got_ids[z] = ids[z]
-    tour = extra_step(1)
-    send_tokens(3)
-    send_tokens(5)
-    for plane in planes:
-        plane.forward()
-    for plane in planes:
-        plane.spread(-1)
-        plane.spread(1)
-
-    tour = extra_step(2)
-    send_tokens(2)
-    send_tokens(6)
 
     lanes = iota((1, 128), 1)
     starts = jnp.full((1, 128), 2**30, I32)
@@ -287,23 +343,12 @@
     for d in range(REACH + 1):
         kdoc[d] = jnp.where(member((chip - d) * CHIP_TOK), 0.0, -BIG).astype(BF16)
 
-    for plane in planes:
-        plane.close()
-        plane.spread(2)
-    last = []
-
-    def pass_on(u):
-        for plane in planes:
-            last.extend(plane.pass_on(u))
-
-    pass_on(0)
-    tour = extra_step(3)
-    send_tokens(1)
-    send_tokens(7)
-    pass_on(-1)
-    pass_on(1)
+    widen(rest)
+    finish(rest)
+    pass_on(rest, 0)
     tour = extra_step(4)
-    pass_on(2)
+    for u in (-1, 1, 2):
+        pass_on(rest, u)
 
     for copy in tokens_sent:
         copy.wait_recv()
@@ -319,15 +364,19 @@
     ]
     own_rows = pl.ds(pl.multiple_of(core * TOK, TOK), TOK)
     other_rows = pl.ds(pl.multiple_of((1 - core) * TOK, TOK), TOK)
-    for part in range(4):
-        cols = slice(part * 512, part * 512 + 512)
+    shared = []
+    for part in range(N_DP):
+        from_z = lax.rem(z + part + N_DP - 1, N_DP)
+        cols = pl.ds(pl.multiple_of(from_z * 256, 256), 256)
         rows = jnp.dot(
-            to_place[0], got[:, :, cols].reshape(TOK, 512), preferred_element_type=F32
+            to_place[0], got[:, :, cols].reshape(TOK, 256), preferred_element_type=F32
         ) + jnp.dot(
-            to_place[1], extra[:, :, cols].reshape(TOK, 512), preferred_element_type=F32
+            to_place[1], extra[:, :, cols].reshape(TOK, 256), preferred_element_type=F32
         )
-        x[own_rows, cols] = rows.astype(BF16)
-    shared = copies.start(x.at[own_rows], x.at[own_rows], partner)
+        x[own_rows, part * 256 : part * 256 + 256] = rows.astype(BF16)
+        if part % 2:
+            ready = x.at[own_rows, part * 256 - 256 : part * 256 + 256]
+            shared.append(copies.start(ready, ready, partner))
     for copy in last:
         copy.wait_recv()
 
@@ -354,7 +403,8 @@
                 kv[2 * g + 1, at] = block.T.astype(BF16)
 
     project_keys(own_rows, core * TOK)
-    shared.wait_recv()
+    for copy in shared:
+        copy.wait_recv()
     project_keys(other_rows, (1 - core) * TOK)
 
     def leg(n, number, d, to, source, when):
@@ -370,42 +420,61 @@
 
     def legs(n):
         own, came = kv.at[n], lambda d: kvbuf.at[d - 1, n]
+        right, left, down = at_chip(0, 1), at_chip(0, -1), at_chip(1, 0)
         inner = (cx == 1) | (cx == 2)
-        return [
-            leg(n, 0, 4, at_chip(1, 0), own, None),
-            leg(n, 1, 1, at_chip(0, 1), own, cx < 3),
-            leg(n, 2, 3, at_chip(0, -1), own, cx == 0),
-            leg(n, 3, 3, at_chip(0, -1), came(4), cx > 0),
-            leg(n, 4, 1, at_chip(0, 1), came(4), cx == 3),
-            leg(n, 5, 2, at_chip(0, 1), came(1), inner),
-            leg(n, 6, 2, at_chip(0, -1), came(3), inner),
-        ]
-
-    routes = [legs(n) for n in range(PIECES)]
-
-    def do(action, n, number):
-        copy, when = routes[n][number]
-        run = copy.start if action == "start" else copy.wait_send
-        if when is None:
-            run()
-        else:
-            pl.when(when)(run)
+        first = [(4, down, own, None), (1, right, own, cx < 3), (3, left, own, cx == 0)]
+        if n < 2:
+            return {
+                0: first,
+                4: [(3, left, came(4), cx > 0), (1, right, came(4), cx == 3)],
+                1: [(2, right, came(1), inner)],
+                3: [(2, left, came(3), inner)],
+            }
+        return {
+            0: first + [(PASSING, left, own, cx == 1)],
+            4: [(3, left, came(4), cx > 1), (1, right, came(4), cx == 3)],
+            1: [(2, right, came(1), cx == 0), (PASSING, down, came(1), cx == 3)],
+            PASSING: [
+                (2, left, came(PASSING), cx == 0),
+                (3, down, came(PASSING), cx == 0),
+                (2, right, came(PASSING), cx == 3),
+            ],
+            3: [(2, left, came(3), cx == 3)],
+        }
+
+    routes, number = [], 0
+    for n in range(PIECES):
+        number = 0
+        route_of = {}
+        for cause, parts in legs(n).items():
+            route_of[cause] = []
+            for d, to, source, when in parts:
+                route_of[cause].append(leg(n, number, d, to, source, when))
+                number += 1
+        routes.append(route_of)
+
+    def do(action, n, cause):
+        for copy, when in routes[n].get(cause, []):
+            run = copy.start if action == "start" else copy.wait_send
+            if when is None:
+                run()
+            else:
+                pl.when(when)(run)
 
     def arrived(n, d):
-        pltpu.make_async_remote_copy(
+        wait = pltpu.make_async_remote_copy(
             src_ref=kvbuf.at[d - 1, n],
             dst_ref=kvbuf.at[d - 1, n],
             send_sem=leg_send.at[n, 0],
             recv_sem=leg_recv.at[n, d - 1],
             device_id=partner,
             device_id_type=MESH,
-        ).wait_recv()
-        for number in {4: (3, 4), 1: (5,), 3: (6,), 2: ()}[d]:
-            do("start", n, number)
+        ).wait_recv
+        wait()
+        do("start", n, d)
 
     for n in range(PIECES):
-        for number in range(3):
-            do("start", n, number)
+        do("start", n, 0)
 
     def query(c, carry):
         for n, part in enumerate(rotated(project(c, slice(0, CHIP_TOK)), slice(0, CHIP_TOK))):
@@ -480,39 +549,30 @@
         cols = slice(g * 512, g * 512 + 512)
         return copies.start(mine.at[other_rows, cols], out.at[:, out_cols(g)], partner)
 
-    for n, d in ((0, 4), (0, 1)):
-        arrived(n, d)
-    attend(0, 0, first=True)
-    for n, d in ((1, 4), (1, 1), (0, 3)):
-        arrived(n, d)
-    attend(0, 1, first=True)
-    for n, d in ((2, 4), (2, 1), (1, 3)):
-        arrived(n, d)
-    attend(4, 0)
-    for n, d in ((3, 4), (3, 1), (2, 3)):
-        arrived(n, d)
-    attend(1, 0)
-    arrived(3, 3)
-    attend(4, 1)
-    attend(1, 1)
-    attend(3, 0)
-    attend(3, 1)
-    arrived(0, 2)
-    arrived(1, 2)
-    attend(2, 0, last=True)
-    back = [give(0)]
-    arrived(2, 2)
-    arrived(3, 2)
-    attend(2, 1, last=True)
-    back.append(give(1))
+    def arrive(step):
+        for column, events in enumerate(ARRIVALS[step]):
+            if events:
+
+                @pl.when(cx == column)
+                def _(events=events):
+                    for n, d in events:
+                        arrived(n, d)
+
+    back = []
+    for step, (d, g) in enumerate(ORDER):
+        arrive(step)
+        attend(d, g, first=d == 0, last=d == 2)
+        if d == 2:
+            back.append(give(g))
     for g in range(2):
         out[:, out_cols(g)] = mine[own_rows, g * 512 : g * 512 + 512]
+    arrive(len(ORDER))
     for copy in back:
         copy.wait_recv()
     copies.drain()
     for n in range(PIECES):
-        for number in range(LEGS):
-            do("wait", n, number)
+        for cause in routes[n]:
+            do("wait", n, cause)
 
 
 def on_device(tokens, qkv_weight, route, offset, doc_lengths):
@@ -520,13 +580,18 @@
     freq = ROPE_BASE ** (-(jnp.arange(half, dtype=F32) * 2.0 / HEAD_SIZE))
     freq = jnp.concatenate([freq, freq])[None]
     vmem = pl.BlockSpec(memory_space=pltpu.VMEM)
+    hbm = pl.BlockSpec(memory_space=pltpu.HBM)
     smem = pl.BlockSpec(memory_space=pltpu.SMEM)
     return pl.pallas_call(
         kernel,
         out_shape=jax.ShapeDtypeStruct((TOK, 2 * QCOLS), BF16),
-        in_specs=[vmem, vmem, vmem, vmem, smem, vmem],
+        in_specs=[hbm, hbm, hbm, hbm, smem, vmem],
         out_specs=vmem,
         scratch_shapes=[
+            pltpu.VMEM((TOK, MODEL), BF16),
+            pltpu.VMEM((8, 2 * COLS), BF16),
+            pltpu.VMEM((1, TOK), I32),
+            pltpu.VMEM((1, TOK), I32),
             pltpu.VMEM((N_DP, SLOT, MODEL), BF16),
             pltpu.VMEM((N_DP, 8, 128), I32),
             pltpu.VMEM((N_DP, SLOT, MODEL), BF16),
@@ -540,7 +605,7 @@
             pltpu.VMEM((CHIP_TOK, HEAD_SIZE), F32),
             pltpu.VMEM((CHIP_TOK, QCOLS), BF16),
             pltpu.VMEM((PIECES, CHIP_TOK, HEAD_SIZE), BF16),
-            pltpu.VMEM((REACH, PIECES, CHIP_TOK, HEAD_SIZE), BF16),
+            pltpu.VMEM((PASSING, PIECES, CHIP_TOK, HEAD_SIZE), BF16),
             pltpu.VMEM((CHIP_TOK, 128), BF16),
             pltpu.VMEM((REACH + 1, CHIP_TOK, 128), BF16),
             pltpu.VMEM((8, 1, CHIP_TOK), F32),
@@ -550,7 +615,8 @@
             pltpu.SemaphoreType.DMA((N_COPIES,)),
             pltpu.SemaphoreType.DMA((N_COPIES,)),
             pltpu.SemaphoreType.DMA((PIECES, LEGS)),
-            pltpu.SemaphoreType.DMA((PIECES, REACH)),
+            pltpu.SemaphoreType.DMA((PIECES, PASSING)),
+            pltpu.SemaphoreType.DMA((4,)),
         ],
         compiler_params=pltpu.CompilerParams(
             collective_id=0, has_side_effects=True, vmem_limit_bytes=50 * 2**20

time: 109 us -> 101 us (0.927)
  Pallas kernels: 105 us -> 97.2 us
    pallas_call x1, Pallas kernels: 105 us -> 97.2 us  [on_device(): pl.pallas_call(kernel, out_shape=jax.ShapeDtypeStruct((TOK, 2 * QCOLS), B...]
where the time goes in v3:
time: 101 us
  Pallas kernels  97.2 us (96%)
  local copies, waits for them, and re-layouts  3.59 us (4%)
    pallas_call x1, Pallas kernels, on_device(): pl.pallas_call(kernel, out_shape=jax.ShapeDtypeStruct((TOK, 2 * QCOLS), B...  97.2 us
    unnamed x11, local copies, waits for them, and re-layouts  3.59 us

profile of v3, /device:TPU:1, one launch (start us, length us, event | category | flops | bytes accessed | tf_op | source)
XLA Modules:
  0.0 100.9 jit_solution(16245835282999439116)
XLA Ops:
  0.0 0.0 copy-start.3
  0.0 0.0 copy-start.2
  0.0 0.0 copy-start.4
  0.0 0.1 maximum_bitcast_fusion.freq
  0.1 0.6 copy-done.3
  0.7 0.0 copy-done.2
  0.7 0.0 copy-done.4
  0.7 0.0 copy-start
  0.7 1.2 %copy-done = bf16[256,2048]{1,0:T(8,128)(2,1)S(1)} copy-done((bf16[256,2048]{1,0:T(8,128)(2,1)S(1)}, bf16[256,2048]{1,0:T(8,128)(2,1)}, u32[]{:S(2)}) %copy-start) | copy-done | bytes 1048600
  1.9 0.0 copy-start.1
  1.9 0.8 copy-done.1
  2.7 97.2 %shard_map.55 = bf16[256,2048]{1,0:T(8,128)(2,1)S(1)} custom-call(bf16[256,2048]{1,0:T(8,128)(2,1)S(1)} %copy-done, bf16[8,3072]{1,0:T(8,128)(2,1)S(1)} %copy-done.1, s32[1,256]{1,0:T(1,128)S(1)} %bitcast.4, s32[1,256]{1,0:T(1,128)S(1)} %bitcast.5, s32[1,16]{1,0:T(1,128)S(1)} %copy-done.4, f32[1,128]{1,0:T(1,128)S(1)} %maximum_bitcast_fusion.freq), custom_call_target="tpu_custom_call" | custom-call | tf_op jit(solution)/shard_map/pallas_call | solution.py:585
  99.9 1.0 copy.7
  (1 shorter events, 0.0 us)
Async XLA Ops:
  0.0 0.7 copy-start.3
  0.0 0.7 copy-start.2
  0.0 0.7 copy-start.4
  0.7 1.2 %copy-start = (bf16[256,2048]{1,0:T(8,128)(2,1)S(1)}, bf16[256,2048]{1,0:T(8,128)(2,1)}, u32[]{:S(2)}) copy-start(bf16[256,2048]{1,0:T(8,128)(2,1)} %tokens_in.1) | copy-start | bytes 3145732
  1.9 0.8 copy-start.1

commit v4 on v3

--- a/solution.py
+++ b/solution.py
@@ -19,9 +19,10 @@
 COLS = QCOLS + 2 * KVCOLS
 HALF = COLS // 2
 REACH = 4
-HEADS_AT_ONCE = 2
+HEADS_AT_ONCE = 4
 DOCS = 16
-PIECES = 4
+PIECES = 8
+CROSSING = (2, 5, 7)
 LEGS = 12
 PASSING = 5
 BIG = 2.0**100
@@ -32,14 +33,14 @@
 ARRIVALS = (
     ((), (), (), ()),
     ((), (), (), ()),
-    (((0, 4), (2, 5), (1, 4), (3, 5),), ((0, 1), (0, 4), (1, 1), (1, 4),), ((0, 1), (0, 4), (1, 1), (1, 4),), ((0, 3), (0, 1), (0, 4), (1, 3), (1, 1), (1, 4),)),
-    (((2, 4), (0, 3), (0, 1), (3, 4), (1, 3), (1, 1),), (), (), ()),
-    (((2, 3),), ((2, 1), (2, 4), (0, 3), (3, 1), (3, 4),), ((2, 1), (2, 4), (0, 3), (3, 1), (3, 4),), ((2, 3), (2, 1), (2, 4), (3, 3), (3, 1), (3, 4),)),
-    (((0, 2), (2, 1), (3, 3), (1, 2), (3, 1),), ((1, 3),), ((1, 3),), ()),
-    ((), ((2, 3),), ((0, 2), (2, 2),), ((0, 2), (2, 2), (2, 5),)),
-    (((2, 2),), ((0, 2), (3, 3),), ((1, 2), (2, 3), (3, 2), (3, 3),), ((1, 2), (3, 2), (3, 5),)),
-    (((3, 2),), ((2, 2), (1, 2),), (), ()),
-    ((), ((3, 2),), (), ()),
+    (((0, 4), (2, 5), (1, 4), (5, 5), (2, 4), (7, 5), (3, 4),), ((0, 1), (0, 4), (1, 1), (1, 4), (2, 1), (2, 4), (3, 1), (3, 4),), ((0, 1), (0, 4), (1, 1), (1, 4), (2, 1), (2, 4), (3, 1), (3, 4),), ((0, 3), (0, 1), (0, 4), (1, 3), (1, 1), (1, 4), (2, 3), (2, 1), (2, 4), (3, 3), (3, 1), (3, 4),)),
+    (((0, 3), (0, 1), (4, 4), (1, 3), (1, 1), (5, 4), (2, 1), (3, 3), (6, 4), (3, 1),), ((0, 3), (4, 1), (4, 4), (1, 3),), ((0, 3), (4, 1), (4, 4), (1, 3),), ((4, 3), (4, 1), (4, 4),)),
+    (((0, 2), (7, 4), (4, 1), (4, 3),), ((5, 1), (5, 4), (2, 3), (6, 1), (6, 4), (3, 3), (7, 1), (7, 4),), ((5, 1), (5, 4), (2, 2), (6, 1), (6, 4), (2, 3), (7, 1), (7, 4),), ((5, 3), (5, 1), (5, 4), (6, 3), (6, 1), (6, 4), (7, 3), (7, 1), (7, 4),)),
+    (((2, 3), (5, 1), (1, 2), (5, 3), (6, 1), (6, 3), (7, 3), (7, 1),), ((0, 2), (2, 2), (4, 3),), ((3, 3), (0, 2),), ((0, 2), (2, 2), (2, 5),)),
+    (((3, 2), (2, 2), (4, 2),), ((1, 2),), ((4, 3), (1, 2), (5, 2),), ((1, 2), (5, 2), (5, 5),)),
+    (((5, 2),), ((5, 3), (6, 3), (5, 2), (7, 3),), ((3, 2), (5, 3), (4, 2), (6, 3), (6, 2), (7, 2), (7, 3),), ((7, 2), (3, 2), (7, 5), (4, 2),)),
+    (((7, 2), (6, 2),), ((7, 2), (3, 2),), (), ((6, 2),)),
+    ((), ((4, 2), (6, 2),), (), ()),
     ((), (), (), ()),
 )
 MESH = pl.DeviceIdType.MESH
@@ -173,6 +174,40 @@
             sent.append(copies.start(wbuf.at[1 + s, chip], wbuf.at[2 + s, chip], at_z(-1)))
         return sent
 
+    facts = jnp.where(
+        group == 0,
+        offset[...] - sp * TOK,
+        jnp.where(group == 1, route_row, jnp.where(group == 2, 1, 0)),
+    ).astype(F32).astype(BF16)
+    lane = iota((TOK, TOK), 0) - z * SLOT
+    lane_ok = jnp.where((lane >= 0) & (lane < SLOT), lane, -10 * TOK)
+
+    def numbers_of(block):
+        pick = (lane_ok + block * SLOT == dest).astype(F32).astype(BF16)
+        found = lax.dot_general(
+            facts, pick, (((1,), (1,)), ((), ())), preferred_element_type=F32
+        ).astype(I32)
+        number = found[1:2] * TOK + found[0:1] + found[2:3]
+        return [number[:, 0:128], number[:, 128:256]]
+
+    more = numbers_of(N_DP) + [jnp.zeros((4, 128), I32)]
+
+    def prepare(d):
+        to = lax.rem(z + d, N_DP)
+        packed[to] = pack(to)
+        ids[to] = jnp.concatenate(numbers_of(to) + more, axis=0)
+
+    tokens_sent = []
+
+    def send_tokens(d):
+        to = lax.rem(z + d, N_DP)
+        tokens_sent.append(copies.start(packed.at[to], got.at[z], at_z(d)))
+        tokens_sent.append(copies.start(ids.at[to], got_ids.at[z], at_z(d)))
+
+    for d in (1, 7):
+        prepare(d)
+        send_tokens(d)
+
     swap.wait_recv()
     for base, width, part in half_of(core):
         own = part.astype(F32)
@@ -182,41 +217,13 @@
         wbuf[1, chip, :, base : base + width] = jnp.concatenate([first, second], axis=0).astype(BF16)
     w_tour = w_ring(0)
 
-    facts = jnp.where(
-        group == 0,
-        offset[...] - sp * TOK,
-        jnp.where(group == 1, route_row, jnp.where(group == 2, 1, 0)),
-    ).astype(F32).astype(BF16)
-    lane = iota((TOK, TOK), 0) - z * SLOT
-    lane_ok = jnp.where((lane >= 0) & (lane < SLOT), lane, -10 * TOK)
-
-    def numbers_of(block):
-        pick = (lane_ok + block * SLOT == dest).astype(F32).astype(BF16)
-        found = lax.dot_general(
-            facts, pick, (((1,), (1,)), ((), ())), preferred_element_type=F32
-        ).astype(I32)
-        number = found[1:2] * TOK + found[0:1] + found[2:3]
-        return [number[:, 0:128], number[:, 128:256]]
-
     extra[z] = pack(N_DP)
-    more = numbers_of(N_DP) + [jnp.zeros((4, 128), I32)]
-
-    def prepare(d):
-        to = lax.rem(z + d, N_DP)
-        packed[to] = pack(to)
-        ids[to] = jnp.concatenate(numbers_of(to) + more, axis=0)
+    tour = extra_ring(0)
 
     def w_step(s):
         for copy in w_tour:
             copy.wait_recv()
         return w_ring(s)
-
-    tokens_sent = []
-
-    def send_tokens(d):
-        to = lax.rem(z + d, N_DP)
-        tokens_sent.append(copies.start(packed.at[to], got.at[z], at_z(d)))
-        tokens_sent.append(copies.start(ids.at[to], got_ids.at[z], at_z(d)))
 
     def extra_step(s):
         for copy in tour:
@@ -288,10 +295,6 @@
         for plane in planes:
             last.extend(plane.pass_on(u))
 
-    tour = extra_ring(0)
-    for d in (1, 7):
-        prepare(d)
-        send_tokens(d)
     w_tour = w_step(1)
     open_plane(near)
     for d in (3, 2):
@@ -402,15 +405,27 @@
                 at = pl.ds(pl.multiple_of(base + t * 128, 128), 128)
                 kv[2 * g + 1, at] = block.T.astype(BF16)
 
+    def queries(rows):
+        def query(c, carry):
+            for n, part in enumerate(rotated(project(c, rows), rows)):
+                q[rows, pl.ds(pl.multiple_of(c * 256 + n * 128, 128), 128)] = part
+            return carry
+
+        lax.fori_loop(0, 4, query, 0)
+
     project_keys(own_rows, core * TOK)
+    queries(own_rows)
     for copy in shared:
         copy.wait_recv()
     project_keys(other_rows, (1 - core) * TOK)
 
+    def piece(n):
+        return n // 2, slice(n % 2 * 256, n % 2 * 256 + 256)
+
     def leg(n, number, d, to, source, when):
         copy = pltpu.make_async_remote_copy(
             src_ref=source,
-            dst_ref=kvbuf.at[d - 1, n],
+            dst_ref=kvbuf.at[(d - 1, *piece(n))],
             send_sem=leg_send.at[n, number],
             recv_sem=leg_recv.at[n, d - 1],
             device_id=to,
@@ -419,11 +434,11 @@
         return copy, when
 
     def legs(n):
-        own, came = kv.at[n], lambda d: kvbuf.at[d - 1, n]
+        own, came = kv.at[piece(n)], lambda d: kvbuf.at[(d - 1, *piece(n))]
         right, left, down = at_chip(0, 1), at_chip(0, -1), at_chip(1, 0)
         inner = (cx == 1) | (cx == 2)
         first = [(4, down, own, None), (1, right, own, cx < 3), (3, left, own, cx == 0)]
-        if n < 2:
+        if n not in CROSSING:
             return {
                 0: first,
                 4: [(3, left, came(4), cx > 0), (1, right, came(4), cx == 3)],
@@ -463,8 +478,8 @@
 
     def arrived(n, d):
         wait = pltpu.make_async_remote_copy(
-            src_ref=kvbuf.at[d - 1, n],
-            dst_ref=kvbuf.at[d - 1, n],
+            src_ref=kvbuf.at[(d - 1, *piece(n))],
+            dst_ref=kvbuf.at[(d - 1, *piece(n))],
             send_sem=leg_send.at[n, 0],
             recv_sem=leg_recv.at[n, d - 1],
             device_id=partner,
@@ -476,12 +491,7 @@
     for n in range(PIECES):
         do("start", n, 0)
 
-    def query(c, carry):
-        for n, part in enumerate(rotated(project(c, slice(0, CHIP_TOK)), slice(0, CHIP_TOK))):
-            q[:, pl.ds(pl.multiple_of(c * 256 + n * 128, 128), 128)] = part
-        return carry
-
-    lax.fori_loop(0, 4, query, 0)
+    queries(other_rows)
 
     def block_step(d, g, heads, first, last):
         keys_of = kv.at[2 * g] if d == 0 else kvbuf.at[d - 1, 2 * g]
@@ -604,8 +614,8 @@
             pltpu.VMEM((CHIP_TOK, HEAD_SIZE), F32),
             pltpu.VMEM((CHIP_TOK, HEAD_SIZE), F32),
             pltpu.VMEM((CHIP_TOK, QCOLS), BF16),
-            pltpu.VMEM((PIECES, CHIP_TOK, HEAD_SIZE), BF16),
-            pltpu.VMEM((PASSING, PIECES, CHIP_TOK, HEAD_SIZE), BF16),
+            pltpu.VMEM((PIECES // 2, CHIP_TOK, HEAD_SIZE), BF16),
+            pltpu.VMEM((PASSING, PIECES // 2, CHIP_TOK, HEAD_SIZE), BF16),
             pltpu.VMEM((CHIP_TOK, 128), BF16),
             pltpu.VMEM((REACH + 1, CHIP_TOK, 128), BF16),
             pltpu.VMEM((8, 1, CHIP_TOK), F32),

time: 101 us -> 95.9 us (0.950)
  Pallas kernels: 97.2 us -> 92 us
    pallas_call x1, Pallas kernels: 97.2 us -> 92 us  [on_device(): pl.pallas_call(kernel, out_shape=jax.ShapeDtypeStruct((TOK, 2 * QCOLS), B...]
where the time goes in v4:
time: 95.9 us; the launch traced here: 95.7 us
  Pallas kernels  92 us (96%)
  local copies, waits for them, and re-layouts  3.59 us (4%)
    pallas_call x1, Pallas kernels, on_device(): pl.pallas_call(kernel, out_shape=jax.ShapeDtypeStruct((TOK, 2 * QCOLS), B...  92 us
    unnamed x11, local copies, waits for them, and re-layouts  3.59 us

profile of v4, /device:TPU:1, one launch (start us, length us, event | category | flops | bytes accessed | tf_op | source)
XLA Modules:
  0.0 95.7 jit_solution(1929630516262690085)
XLA Ops:
  0.0 0.0 copy-start.3
  0.0 0.0 copy-start.2
  0.0 0.0 copy-start.4
  0.0 0.1 maximum_bitcast_fusion.freq
  0.1 0.6 copy-done.3
  0.7 0.0 copy-done.2
  0.7 0.0 copy-done.4
  0.7 0.0 copy-start
  0.7 1.2 %copy-done = bf16[256,2048]{1,0:T(8,128)(2,1)S(1)} copy-done((bf16[256,2048]{1,0:T(8,128)(2,1)S(1)}, bf16[256,2048]{1,0:T(8,128)(2,1)}, u32[]{:S(2)}) %copy-start) | copy-done | bytes 1048600
  1.9 0.0 copy-start.1
  1.9 0.8 copy-done.1
  2.7 92.0 %shard_map.55 = bf16[256,2048]{1,0:T(8,128)(2,1)S(1)} custom-call(bf16[256,2048]{1,0:T(8,128)(2,1)S(1)} %copy-done, bf16[8,3072]{1,0:T(8,128)(2,1)S(1)} %copy-done.1, s32[1,256]{1,0:T(1,128)S(1)} %bitcast.4, s32[1,256]{1,0:T(1,128)S(1)} %bitcast.5, s32[1,16]{1,0:T(1,128)S(1)} %copy-done.4, f32[1,128]{1,0:T(1,128)S(1)} %maximum_bitcast_fusion.freq), custom_call_target="tpu_custom_call" | custom-call | tf_op jit(solution)/shard_map/pallas_call | solution.py:595
  94.8 1.0 %copy.7 = bf16[256,2048]{1,0:T(8,128)(2,1)} copy(bf16[256,2048]{1,0:T(8,128)(2,1)S(1)} %shard_map.55) | data formatting | bytes 2097152
  (1 shorter events, 0.0 us)
Async XLA Ops:
  0.0 0.7 copy-start.3
  0.0 0.7 copy-start.2
  0.0 0.7 copy-start.4
  0.7 1.2 %copy-start = (bf16[256,2048]{1,0:T(8,128)(2,1)S(1)}, bf16[256,2048]{1,0:T(8,128)(2,1)}, u32[]{:S(2)}) copy-start(bf16[256,2048]{1,0:T(8,128)(2,1)} %tokens_in.1) | copy-start | bytes 3145732
  1.9 0.8 copy-start.1

commit v5 on v4

--- a/solution.py
+++ b/solution.py
@@ -29,18 +29,19 @@
 FACTOR = HEAD_SIZE ** (-0.5) * 1.4426950408889634
 EXTRA_RIGHT, EXTRA_LEFT = 4, 3
 W_RIGHT, W_LEFT = 3, 4
-ORDER = ((0, 0), (0, 1), (4, 0), (1, 0), (4, 1), (1, 1), (3, 0), (3, 1), (2, 0), (2, 1))
+PIECE_ORDER = (0, 3, 2, 1, 4, 6, 7, 5)
+ORDER = ((0, 0), (4, 0), (0, 1), (1, 0), (4, 1), (3, 0), (1, 1), (2, 0), (3, 1), (2, 1))
 ARRIVALS = (
     ((), (), (), ()),
-    ((), (), (), ()),
-    (((0, 4), (2, 5), (1, 4), (5, 5), (2, 4), (7, 5), (3, 4),), ((0, 1), (0, 4), (1, 1), (1, 4), (2, 1), (2, 4), (3, 1), (3, 4),), ((0, 1), (0, 4), (1, 1), (1, 4), (2, 1), (2, 4), (3, 1), (3, 4),), ((0, 3), (0, 1), (0, 4), (1, 3), (1, 1), (1, 4), (2, 3), (2, 1), (2, 4), (3, 3), (3, 1), (3, 4),)),
-    (((0, 3), (0, 1), (4, 4), (1, 3), (1, 1), (5, 4), (2, 1), (3, 3), (6, 4), (3, 1),), ((0, 3), (4, 1), (4, 4), (1, 3),), ((0, 3), (4, 1), (4, 4), (1, 3),), ((4, 3), (4, 1), (4, 4),)),
-    (((0, 2), (7, 4), (4, 1), (4, 3),), ((5, 1), (5, 4), (2, 3), (6, 1), (6, 4), (3, 3), (7, 1), (7, 4),), ((5, 1), (5, 4), (2, 2), (6, 1), (6, 4), (2, 3), (7, 1), (7, 4),), ((5, 3), (5, 1), (5, 4), (6, 3), (6, 1), (6, 4), (7, 3), (7, 1), (7, 4),)),
-    (((2, 3), (5, 1), (1, 2), (5, 3), (6, 1), (6, 3), (7, 3), (7, 1),), ((0, 2), (2, 2), (4, 3),), ((3, 3), (0, 2),), ((0, 2), (2, 2), (2, 5),)),
-    (((3, 2), (2, 2), (4, 2),), ((1, 2),), ((4, 3), (1, 2), (5, 2),), ((1, 2), (5, 2), (5, 5),)),
-    (((5, 2),), ((5, 3), (6, 3), (5, 2), (7, 3),), ((3, 2), (5, 3), (4, 2), (6, 3), (6, 2), (7, 2), (7, 3),), ((7, 2), (3, 2), (7, 5), (4, 2),)),
-    (((7, 2), (6, 2),), ((7, 2), (3, 2),), (), ((6, 2),)),
-    ((), ((4, 2), (6, 2),), (), ()),
+    (((0, 4), (2, 5), (3, 4), (7, 5), (2, 4), (5, 5), (0, 1), (1, 4), (0, 3),), ((0, 1), (0, 4), (3, 1), (3, 4), (2, 1), (2, 4), (0, 3), (1, 1), (1, 4),), ((0, 1), (0, 4), (3, 1), (3, 4), (2, 1), (2, 4), (0, 3), (1, 1), (1, 4),), ((0, 3), (0, 1), (0, 4), (3, 3), (3, 1), (3, 4), (2, 3), (2, 1), (2, 4), (1, 3), (1, 1), (1, 4),)),
+    (((3, 1), (4, 4), (3, 3),), ((3, 3), (4, 1), (4, 4),), ((3, 3), (4, 1), (4, 4),), ((4, 3), (4, 1), (4, 4),)),
+    (((2, 1), (6, 4), (0, 2), (1, 1),), ((2, 3), (6, 1), (6, 4),), ((2, 2), (6, 1), (6, 4),), ((6, 3), (6, 1), (6, 4),)),
+    (((7, 4), (1, 3), (4, 1), (5, 4), (3, 2),), ((0, 2), (7, 1), (7, 4), (1, 3), (5, 1), (5, 4),), ((2, 3), (7, 1), (7, 4), (1, 3), (5, 1), (5, 4),), ((7, 3), (7, 1), (7, 4), (5, 3), (5, 1), (5, 4),)),
+    (((2, 3), (6, 1), (4, 3),), ((3, 2), (2, 2),), ((4, 3), (0, 2),), ((0, 2), (2, 2), (2, 5),)),
+    (((7, 3), (6, 3), (7, 1), (5, 3), (1, 2), (5, 1),), ((4, 3),), ((6, 3), (3, 2),), ((3, 2), (7, 2), (7, 5),)),
+    (((2, 2),), ((6, 3), (7, 3), (1, 2),), ((7, 2), (1, 2), (7, 3), (4, 2),), ((5, 2), (1, 2), (5, 5), (4, 2),)),
+    (((4, 2), (7, 2),), ((7, 2), (5, 3),), ((5, 2), (6, 2), (5, 3),), ((6, 2),)),
+    (((6, 2), (5, 2),), ((5, 2), (4, 2), (6, 2),), (), ()),
     ((), (), (), ()),
 )
 MESH = pl.DeviceIdType.MESH
@@ -488,7 +489,7 @@
         wait()
         do("start", n, d)
 
-    for n in range(PIECES):
+    for n in PIECE_ORDER:
         do("start", n, 0)
 
     queries(other_rows)

time: 95.9 us -> 94.6 us (0.986)
  Pallas kernels: 92 us -> 90.7 us
    pallas_call x1, Pallas kernels: 92 us -> 90.7 us  [on_device(): pl.pallas_call(kernel, out_shape=jax.ShapeDtypeStruct((TOK, 2 * QCOLS), B...]
where the time goes in v5:
time: 94.6 us; the launch traced here: 94.4 us
  Pallas kernels  90.7 us (96%)
  local copies, waits for them, and re-layouts  3.59 us (4%)
    pallas_call x1, Pallas kernels, on_device(): pl.pallas_call(kernel, out_shape=jax.ShapeDtypeStruct((TOK, 2 * QCOLS), B...  90.7 us
    unnamed x11, local copies, waits for them, and re-layouts  3.59 us

profile of v5, /device:TPU:1, one launch (start us, length us, event | category | flops | bytes accessed | tf_op | source)
XLA Modules:
  0.0 94.4 jit_solution(5224371361819438891)
XLA Ops:
  0.0 0.0 copy-start.3
  0.0 0.0 copy-start.2
  0.0 0.0 copy-start.4
  0.0 0.1 maximum_bitcast_fusion.freq
  0.1 0.6 copy-done.3
  0.7 0.0 copy-done.2
  0.7 0.0 copy-done.4
  0.7 0.0 copy-start
  0.7 1.2 %copy-done = bf16[256,2048]{1,0:T(8,128)(2,1)S(1)} copy-done((bf16[256,2048]{1,0:T(8,128)(2,1)S(1)}, bf16[256,2048]{1,0:T(8,128)(2,1)}, u32[]{:S(2)}) %copy-start) | copy-done | bytes 1048600
  1.9 0.0 copy-start.1
  1.9 0.8 copy-done.1
  2.7 90.7 %shard_map.55 = bf16[256,2048]{1,0:T(8,128)(2,1)S(1)} custom-call(bf16[256,2048]{1,0:T(8,128)(2,1)S(1)} %copy-done, bf16[8,3072]{1,0:T(8,128)(2,1)S(1)} %copy-done.1, s32[1,256]{1,0:T(1,128)S(1)} %bitcast.4, s32[1,256]{1,0:T(1,128)S(1)} %bitcast.5, s32[1,16]{1,0:T(1,128)S(1)} %copy-done.4, f32[1,128]{1,0:T(1,128)S(1)} %maximum_bitcast_fusion.freq), custom_call_target="tpu_custom_call" | custom-call | tf_op jit(solution)/shard_map/pallas_call | solution.py:596
  93.4 1.0 %copy.7 = bf16[256,2048]{1,0:T(8,128)(2,1)} copy(bf16[256,2048]{1,0:T(8,128)(2,1)S(1)} %shard_map.55) | data formatting | bytes 2097152
  (1 shorter events, 0.0 us)
Async XLA Ops:
  0.0 0.7 copy-start.3
  0.0 0.7 copy-start.2
  0.0 0.7 copy-start.4
  0.7 1.2 %copy-start = (bf16[256,2048]{1,0:T(8,128)(2,1)S(1)}, bf16[256,2048]{1,0:T(8,128)(2,1)}, u32[]{:S(2)}) copy-start(bf16[256,2048]{1,0:T(8,128)(2,1)} %tokens_in.1) | copy-start | bytes 3145732
  1.9 0.8 copy-start.1

commit v6 on v4

--- a/solution.py
+++ b/solution.py
@@ -22,25 +22,26 @@
 HEADS_AT_ONCE = 4
 DOCS = 16
 PIECES = 8
-CROSSING = (2, 5, 7)
+CROSSING = (1, 3, 5)
 LEGS = 12
 PASSING = 5
 BIG = 2.0**100
 FACTOR = HEAD_SIZE ** (-0.5) * 1.4426950408889634
 EXTRA_RIGHT, EXTRA_LEFT = 4, 3
 W_RIGHT, W_LEFT = 3, 4
-ORDER = ((0, 0), (0, 1), (4, 0), (1, 0), (4, 1), (1, 1), (3, 0), (3, 1), (2, 0), (2, 1))
+PIECE_ORDER = (0, 2, 4, 6, 1, 3, 7, 5)
+ORDER = ((0, 1), (0, 0), (4, 0), (4, 1), (1, 0), (3, 0), (1, 1), (2, 0), (3, 1), (2, 1))
 ARRIVALS = (
-    ((), (), (), ()),
-    ((), (), (), ()),
-    (((0, 4), (2, 5), (1, 4), (5, 5), (2, 4), (7, 5), (3, 4),), ((0, 1), (0, 4), (1, 1), (1, 4), (2, 1), (2, 4), (3, 1), (3, 4),), ((0, 1), (0, 4), (1, 1), (1, 4), (2, 1), (2, 4), (3, 1), (3, 4),), ((0, 3), (0, 1), (0, 4), (1, 3), (1, 1), (1, 4), (2, 3), (2, 1), (2, 4), (3, 3), (3, 1), (3, 4),)),
-    (((0, 3), (0, 1), (4, 4), (1, 3), (1, 1), (5, 4), (2, 1), (3, 3), (6, 4), (3, 1),), ((0, 3), (4, 1), (4, 4), (1, 3),), ((0, 3), (4, 1), (4, 4), (1, 3),), ((4, 3), (4, 1), (4, 4),)),
-    (((0, 2), (7, 4), (4, 1), (4, 3),), ((5, 1), (5, 4), (2, 3), (6, 1), (6, 4), (3, 3), (7, 1), (7, 4),), ((5, 1), (5, 4), (2, 2), (6, 1), (6, 4), (2, 3), (7, 1), (7, 4),), ((5, 3), (5, 1), (5, 4), (6, 3), (6, 1), (6, 4), (7, 3), (7, 1), (7, 4),)),
-    (((2, 3), (5, 1), (1, 2), (5, 3), (6, 1), (6, 3), (7, 3), (7, 1),), ((0, 2), (2, 2), (4, 3),), ((3, 3), (0, 2),), ((0, 2), (2, 2), (2, 5),)),
-    (((3, 2), (2, 2), (4, 2),), ((1, 2),), ((4, 3), (1, 2), (5, 2),), ((1, 2), (5, 2), (5, 5),)),
-    (((5, 2),), ((5, 3), (6, 3), (5, 2), (7, 3),), ((3, 2), (5, 3), (4, 2), (6, 3), (6, 2), (7, 2), (7, 3),), ((7, 2), (3, 2), (7, 5), (4, 2),)),
-    (((7, 2), (6, 2),), ((7, 2), (3, 2),), (), ((6, 2),)),
-    ((), ((4, 2), (6, 2),), (), ()),
+    (((0, 4), (2, 4),), ((0, 1), (0, 4), (2, 1), (2, 4),), ((0, 1), (0, 4), (2, 1), (2, 4),), ((0, 3), (0, 1), (0, 4), (2, 3), (2, 1), (2, 4),)),
+    (((4, 4), (1, 5),), ((4, 1), (4, 4),), ((4, 1), (4, 4),), ((4, 3), (4, 1), (4, 4),)),
+    (((0, 1), (6, 4), (3, 5), (1, 4), (2, 1), (5, 5), (3, 4), (0, 3),), ((0, 3), (6, 1), (6, 4), (2, 3), (1, 1), (1, 4), (4, 3), (3, 1), (3, 4),), ((0, 3), (6, 1), (6, 4), (1, 1), (1, 4), (2, 3), (3, 1), (3, 4),), ((6, 3), (6, 1), (6, 4), (1, 3), (1, 1), (1, 4), (3, 3), (3, 1), (3, 4),)),
+    (((4, 1), (7, 4), (2, 3), (6, 1), (5, 4), (4, 3),), ((0, 2), (7, 1), (7, 4), (6, 3), (5, 1), (5, 4),), ((4, 3), (7, 1), (7, 4), (6, 3), (5, 1), (5, 4),), ((7, 3), (7, 1), (7, 4), (5, 3), (5, 1), (5, 4),)),
+    (((1, 1), (1, 3), (0, 2), (3, 1),), ((1, 3),), ((1, 2), (0, 2),), ((0, 2), (1, 2), (1, 5),)),
+    (((3, 3), (6, 3), (7, 1),), ((2, 2), (3, 3),), ((1, 3), (2, 2), (3, 2), (4, 2), (3, 3),), ((2, 2), (3, 2), (3, 5),)),
+    (((5, 3), (2, 2), (5, 1), (4, 2), (1, 2),), ((1, 2), (4, 2),), ((6, 2), (7, 3),), ((4, 2), (5, 2), (5, 5), (6, 2),)),
+    (((7, 3), (3, 2),), ((3, 2), (7, 3),), ((7, 2), (5, 2),), ((7, 2),)),
+    (((6, 2), (5, 2),), ((6, 2), (5, 2), (5, 3),), ((5, 3),), ()),
+    (((7, 2),), ((7, 2),), (), ()),
     ((), (), (), ()),
 )
 MESH = pl.DeviceIdType.MESH
@@ -413,14 +414,8 @@
 
         lax.fori_loop(0, 4, query, 0)
 
-    project_keys(own_rows, core * TOK)
-    queries(own_rows)
-    for copy in shared:
-        copy.wait_recv()
-    project_keys(other_rows, (1 - core) * TOK)
-
     def piece(n):
-        return n // 2, slice(n % 2 * 256, n % 2 * 256 + 256)
+        return n // 2, (own_rows, other_rows)[n % 2]
 
     def leg(n, number, d, to, source, when):
         copy = pltpu.make_async_remote_copy(
@@ -488,9 +483,16 @@
         wait()
         do("start", n, d)
 
-    for n in range(PIECES):
+    project_keys(own_rows, core * TOK)
+    for n in PIECE_ORDER[:4]:
         do("start", n, 0)
-
+    queries(own_rows)
+    for copy in shared:
+        copy.wait_recv()
+    project_keys(other_rows, (1 - core) * TOK)
+
+    for n in PIECE_ORDER[4:]:
+        do("start", n, 0)
     queries(other_rows)
 
     def block_step(d, g, heads, first, last):

time: 95.9 us -> 93.9 us (0.979)
  Pallas kernels: 92 us -> 90 us
    pallas_call x1, Pallas kernels: 92 us -> 90 us  [on_device(): pl.pallas_call(kernel, out_shape=jax.ShapeDtypeStruct((TOK, 2 * QCOLS), B...]
where the time goes in v6:
time: 93.9 us; the launch traced here: 93.7 us
  Pallas kernels  90 us (96%)
  local copies, waits for them, and re-layouts  3.59 us (4%)
    pallas_call x1, Pallas kernels, on_device(): pl.pallas_call(kernel, out_shape=jax.ShapeDtypeStruct((TOK, 2 * QCOLS), B...  90 us
    unnamed x11, local copies, waits for them, and re-layouts  3.59 us

profile of v6, /device:TPU:1, one launch (start us, length us, event | category | flops | bytes accessed | tf_op | source)
XLA Modules:
  0.0 93.7 jit_solution(6973553091923701313)
XLA Ops:
  0.0 0.0 copy-start.3
  0.0 0.0 copy-start.2
  0.0 0.0 copy-start.4
  0.0 0.1 maximum_bitcast_fusion.freq
  0.1 0.6 copy-done.3
  0.7 0.0 copy-done.2
  0.7 0.0 copy-done.4
  0.7 0.0 copy-start
  0.7 1.2 %copy-done = bf16[256,2048]{1,0:T(8,128)(2,1)S(1)} copy-done((bf16[256,2048]{1,0:T(8,128)(2,1)S(1)}, bf16[256,2048]{1,0:T(8,128)(2,1)}, u32[]{:S(2)}) %copy-start) | copy-done | bytes 1048600
  1.9 0.0 copy-start.1
  1.9 0.8 copy-done.1
  2.7 90.0 %shard_map.55 = bf16[256,2048]{1,0:T(8,128)(2,1)S(1)} custom-call(bf16[256,2048]{1,0:T(8,128)(2,1)S(1)} %copy-done, bf16[8,3072]{1,0:T(8,128)(2,1)S(1)} %copy-done.1, s32[1,256]{1,0:T(1,128)S(1)} %bitcast.4, s32[1,256]{1,0:T(1,128)S(1)} %bitcast.5, s32[1,16]{1,0:T(1,128)S(1)} %copy-done.4, f32[1,128]{1,0:T(1,128)S(1)} %maximum_bitcast_fusion.freq), custom_call_target="tpu_custom_call" | custom-call | tf_op jit(solution)/shard_map/pallas_call | solution.py:597
  92.7 1.0 %copy.7 = bf16[256,2048]{1,0:T(8,128)(2,1)} copy(bf16[256,2048]{1,0:T(8,128)(2,1)S(1)} %shard_map.55) | data formatting | bytes 2097152
  (1 shorter events, 0.0 us)
Async XLA Ops:
  0.0 0.7 copy-start.3
  0.0 0.7 copy-start.2
  0.0 0.7 copy-start.4
  0.7 1.2 %copy-start = (bf16[256,2048]{1,0:T(8,128)(2,1)S(1)}, bf16[256,2048]{1,0:T(8,128)(2,1)}, u32[]{:S(2)}) copy-start(bf16[256,2048]{1,0:T(8,128)(2,1)} %tokens_in.1) | copy-start | bytes 3145732
  1.9 0.8 copy-start.1

commit v7 on v6

--- a/solution.py
+++ b/solution.py
@@ -88,11 +88,10 @@
 
 
 def kernel(
-    tokens_in, w_in, route_in, offset_in, lens, freq, out,
-    tokens, w, route, offset,
+    tokens, w, route, offset, lens, freq, out,
     packed, ids, got, got_ids, extra, wsend, wrecv, wbuf, x,
     cosine, sine, q, kv, kvbuf, qdoc, kdoc, top, total, acc, mine,
-    send, recv, leg_send, leg_recv, load,
+    send, recv, leg_send, leg_recv,
 ):
     z = lax.axis_index("dp")
     sp = lax.axis_index("sp")
@@ -123,15 +122,6 @@
         + [partner]
         + [at_chip(0, 1), at_chip(0, -1), at_chip(1, 0), at_chip(-1, 0)]
     )
-    loads = [
-        pltpu.make_async_copy(here, there, load.at[n])
-        for n, (here, there) in enumerate(
-            [(w_in, w), (route_in, route), (offset_in, offset), (tokens_in, tokens)]
-        )
-    ]
-    for copy in loads:
-        copy.start()
-    loads[0].wait()
     for base, width, part in half_of(1 - core):
         wsend[:, base : base + width] = part.astype(F32)
 
@@ -139,9 +129,6 @@
     copies = Copies(send, recv)
 
     swap = copies.start(wsend, wrecv, partner)
-
-    for copy in loads[1:]:
-        copy.wait()
 
     group = iota((8, TOK), 0)
     route_row = route[...]
@@ -592,18 +579,13 @@
     freq = ROPE_BASE ** (-(jnp.arange(half, dtype=F32) * 2.0 / HEAD_SIZE))
     freq = jnp.concatenate([freq, freq])[None]
     vmem = pl.BlockSpec(memory_space=pltpu.VMEM)
-    hbm = pl.BlockSpec(memory_space=pltpu.HBM)
     smem = pl.BlockSpec(memory_space=pltpu.SMEM)
     return pl.pallas_call(
         kernel,
         out_shape=jax.ShapeDtypeStruct((TOK, 2 * QCOLS), BF16),
-        in_specs=[hbm, hbm, hbm, hbm, smem, vmem],
+        in_specs=[vmem, vmem, vmem, vmem, smem, vmem],
         out_specs=vmem,
         scratch_shapes=[
-            pltpu.VMEM((TOK, MODEL), BF16),
-            pltpu.VMEM((8, 2 * COLS), BF16),
-            pltpu.VMEM((1, TOK), I32),
-            pltpu.VMEM((1, TOK), I32),
             pltpu.VMEM((N_DP, SLOT, MODEL), BF16),
             pltpu.VMEM((N_DP, 8, 128), I32),
             pltpu.VMEM((N_DP, SLOT, MODEL), BF16),
@@ -628,7 +610,6 @@
             pltpu.SemaphoreType.DMA((N_COPIES,)),
             pltpu.SemaphoreType.DMA((PIECES, LEGS)),
             pltpu.SemaphoreType.DMA((PIECES, PASSING)),
-            pltpu.SemaphoreType.DMA((4,)),
         ],
         compiler_params=pltpu.CompilerParams(
             collective_id=0, has_side_effects=True, vmem_limit_bytes=50 * 2**20

time: 93.9 us -> 93.9 us (level)
  no operation moved by 1% of the time
where the time goes in v7:
time: 93.9 us; the launch traced here: 93.7 us
  Pallas kernels  90 us (96%)
  local copies, waits for them, and re-layouts  3.59 us (4%)
    pallas_call x1, Pallas kernels, on_device(): pl.pallas_call(kernel, out_shape=jax.ShapeDtypeStruct((TOK, 2 * QCOLS), B...  90 us
    unnamed x11, local copies, waits for them, and re-layouts  3.59 us

profile of v7, /device:TPU:1, one launch (start us, length us, event | category | flops | bytes accessed | tf_op | source)
XLA Modules:
  0.0 93.7 jit_solution(16514635686720428541)
XLA Ops:
  0.0 0.0 copy-start.3
  0.0 0.0 copy-start.2
  0.0 0.0 copy-start.4
  0.0 0.1 maximum_bitcast_fusion.freq
  0.1 0.6 copy-done.3
  0.7 0.0 copy-done.2
  0.7 0.0 copy-done.4
  0.7 0.0 copy-start
  0.7 1.2 %copy-done = bf16[256,2048]{1,0:T(8,128)(2,1)S(1)} copy-done((bf16[256,2048]{1,0:T(8,128)(2,1)S(1)}, bf16[256,2048]{1,0:T(8,128)(2,1)}, u32[]{:S(2)}) %copy-start) | copy-done | bytes 1048600
  1.9 0.0 copy-start.1
  1.9 0.8 copy-done.1
  2.7 90.0 %shard_map.55 = bf16[256,2048]{1,0:T(8,128)(2,1)S(1)} custom-call(bf16[256,2048]{1,0:T(8,128)(2,1)S(1)} %copy-done, bf16[8,3072]{1,0:T(8,128)(2,1)S(1)} %copy-done.1, s32[1,256]{1,0:T(1,128)S(1)} %bitcast.4, s32[1,256]{1,0:T(1,128)S(1)} %bitcast.5, s32[1,16]{1,0:T(1,128)S(1)} %copy-done.4, f32[1,128]{1,0:T(1,128)S(1)} %maximum_bitcast_fusion.freq), custom_call_target="tpu_custom_call" | custom-call | tf_op jit(solution)/shard_map/pallas_call | solution.py:583
  92.7 1.0 %copy.7 = bf16[256,2048]{1,0:T(8,128)(2,1)} copy(bf16[256,2048]{1,0:T(8,128)(2,1)S(1)} %shard_map.55) | data formatting | bytes 2097152
  (1 shorter events, 0.0 us)
Async XLA Ops:
  0.0 0.7 copy-start.3
  0.0 0.7 copy-start.2
  0.0 0.7 copy-start.4
  0.7 1.2 %copy-start = (bf16[256,2048]{1,0:T(8,128)(2,1)S(1)}, bf16[256,2048]{1,0:T(8,128)(2,1)}, u32[]{:S(2)}) copy-start(bf16[256,2048]{1,0:T(8,128)(2,1)} %tokens.1) | copy-start | bytes 3145732
  1.9 0.8 copy-start.1
